TPU v7x, 256 devices: a whole 4x4x8 slice. The times are simulated.
256 devices in a mesh: seq: 32 (over z_hi, x, core), chan: 8 (over z_lo, y).
Axes of the slice: x: 4, y: 4, z: 8 (z_hi: 4, z_lo: 2; z = z_hi * 2 + z_lo), core: 2. Of those that a mesh axis runs over, the one named last changes fastest.
Arguments:
- inputs: bfloat16 [4096, 4096], P(('seq', 'chan')), may hold values from -6 to 6
- grad_output: bfloat16 [4096, 4096], P(('seq', 'chan')), may hold values from -0.09375 to 0.09375
- filter_taps: float32 [384, 4096], P('seq', 'chan'), may hold values from -18.973665 to 18.973665
Outputs:
- grad_inputs: bfloat16 [4096, 4096], P(('seq', 'chan'))
- grad_filter: float32 [384, 4096], P('seq', 'chan')
All inputs are finite; a program needn't handle non-finite values.
Results may differ from a plain program's by a relative error of at most 0.001.
Values may be sent and summed in bfloat16 or wider, within the bound.
A program may use at most 64 MiB of HBM per device.

v0:
```python
import functools

import jax
import jax.numpy as jnp
from jax import lax
from jax.experimental import pallas as pl
from jax.experimental.pallas import tpu as pltpu
from jax.sharding import PartitionSpec as P

MESH = pl.DeviceIdType.MESH
F32 = jnp.float32
BF16 = jnp.bfloat16
LANES = 128
CORES = 2

G_ONE, X_ONE, TAPS, G_TWO, X_TWO, GI_TWO, GI_ONE, GF = range(8)


def contract(lhs, rhs, lhs_dim, rhs_dim):
    return lax.dot_general(
        lhs, rhs, (((lhs_dim,), (rhs_dim,)), ((), ())), preferred_element_type=F32
    )


def swap_chunks(tile):
    row = lax.broadcasted_iota(jnp.int32, tile.shape, 0)
    chunk = lax.broadcasted_iota(jnp.int32, tile.shape, 1) // 16
    for bit in (1, 2, 4):
        row_set = (row & bit) != 0
        chunk_set = (chunk & bit) != 0
        below = pltpu.roll(pltpu.roll(tile, 8 - bit, 0), 16 * bit, 1)
        above = pltpu.roll(pltpu.roll(tile, bit, 0), LANES - 16 * bit, 1)
        moved = jnp.where(chunk_set, below, above)
        tile = jnp.where(row_set == chunk_set, tile, moved)
    return tile


def kernel(
    x_hbm, g_hbm, taps_ref, gi_out, gf_out,
    g_one, x_one, g_send, x_send, g_two, x_two,
    tap_send, tap_recv, tap_rows, tap_tiles, toeplitz,
    g_wide, x_wide, g_cat, gi_wide, gi_send, gi_two, gi_turn,
    gf_tiles, gf_rows, gf_send, gf_recv,
    send_sem, recv_sem,
):
    seqs = lax.axis_size("seq")
    chans = lax.axis_size("chan")
    seq = lax.axis_index("seq")
    chan = lax.axis_index("chan")
    core = lax.rem(seq, CORES)
    block = lax.div(seq, CORES)
    blocks = seqs // CORES
    near = core * chans + chan
    nears = CORES * chans
    column = core * blocks + block
    width = g_one.shape[2]

    barrier = pltpu.get_barrier_semaphore()

    def greet_seq(step, carry):
        pl.semaphore_signal(
            barrier, inc=1, device_id={"seq": lax.rem(seq + step, seqs), "chan": chan}, device_id_type=MESH
        )
        return carry

    def greet_near(step, carry):
        other = lax.rem(chan + step, chans)
        for other_core in range(CORES):
            pl.semaphore_signal(
                barrier, inc=1, device_id={"seq": block * CORES + other_core, "chan": other}, device_id_type=MESH
            )
        return carry

    lax.fori_loop(1, chans, greet_near, 0)
    lax.fori_loop(1, seqs, greet_seq, 0)

    lags = taps_ref.shape[0]
    for tile in range(taps_ref.shape[1] // LANES):
        lanes = slice(tile * LANES, (tile + 1) * LANES)
        first = swap_chunks(taps_ref[0:8, lanes])
        last = jnp.concatenate([taps_ref[8:lags, lanes], jnp.zeros((16 - lags, LANES), F32)], axis=0)
        last = swap_chunks(last)
        tap_send[8 * tile : 8 * tile + 8, 0, :] = first
        tap_send[8 * tile : 8 * tile + 8, 1, :] = last

    row = lax.broadcasted_iota(jnp.int32, (width, width), 0)
    lane = lax.broadcasted_iota(jnp.int32, (width, width), 1)
    eye = (row == lane).astype(F32).astype(BF16)
    flip = ((row ^ lane) == LANES - 1).astype(F32).astype(BF16)

    pl.semaphore_wait(barrier, seqs - 1 + CORES * (chans - 1))

    def remote(src, dst, which, to_seq, to_chan):
        pltpu.make_async_remote_copy(
            src_ref=src, dst_ref=dst, send_sem=send_sem.at[which], recv_sem=recv_sem.at[which],
            device_id={"seq": to_seq, "chan": to_chan}, device_id_type=MESH,
        ).start()

    def local(src, dst, which):
        pltpu.make_async_copy(src, dst, recv_sem.at[which]).start()

    def received(ref, which):
        pltpu.make_async_copy(ref, ref, recv_sem.at[which]).wait()

    def sent(ref, which):
        part = ref.at[pl.ds(0, ref.shape[0] - 1)]
        pltpu.make_async_copy(part, part, send_sem.at[which]).wait()

    def columns_of(ref, index):
        other_core = lax.div(index, chans)
        other_chan = lax.rem(index, chans)
        start = pl.multiple_of(other_chan * (CORES * width) + other_core * width, width)
        return ref.at[:, pl.ds(start, width)]

    def to_near(src_of, dst, which):
        def step(shift, carry):
            index = lax.rem(near + shift, nears)
            remote(src_of(index), dst, which, block * CORES + lax.div(index, chans), lax.rem(index, chans))
            return carry

        lax.fori_loop(1, nears, step, 0)
        local(src_of(near), dst, which)

    def to_far(src, dst, which):
        def step(shift, carry):
            index = lax.rem(block + shift, blocks)
            remote(src.at[index], dst.at[block], which, index * CORES + core, chan)
            return carry

        lax.fori_loop(1, blocks, step, 0)
        local(src.at[block], dst.at[block], which)

    to_near(functools.partial(columns_of, g_hbm), g_one.at[near], G_ONE)

    def send_taps(step, carry):
        index = lax.rem(seq + step, seqs)
        slot = lax.rem(index, CORES) * blocks + lax.div(index, CORES)
        remote(tap_send.at[slot], tap_recv.at[seq], TAPS, index, chan)
        return carry

    lax.fori_loop(1, seqs, send_taps, 0)
    local(tap_send.at[column], tap_recv.at[seq], TAPS)
    to_near(functools.partial(columns_of, x_hbm), x_one.at[near], X_ONE)

    received(g_one, G_ONE)
    turned = contract(eye, g_one[...].reshape(width, width), 1, 1)
    g_send[...] = turned.astype(BF16).reshape(g_send.shape)
    to_far(g_send, g_two, G_TWO)

    received(x_one, X_ONE)
    turned = contract(eye, x_one[...].reshape(width, width), 1, 1).astype(BF16)
    turned = contract(turned, flip, 1, 0)
    x_send[...] = turned.astype(BF16).reshape(x_send.shape)
    to_far(x_send, x_two, X_TWO)

    received(tap_recv, TAPS)
    for part in range(2):
        rows = tap_recv[:, part, :]
        for lag in range(8 if part == 0 else lags - 8):
            shifted = rows if lag == 0 else pltpu.roll(rows, LANES - 16 * lag, 1)
            tap_rows[pl.ds(8 * part + lag, seqs, stride=lags), :] = shifted
    tap_count = tap_rows.shape[0] // LANES
    group = tap_tiles.shape[1]
    for tile in range(tap_count):
        tap_tiles[tile] = tap_rows[tile * LANES : (tile + 1) * LANES, :].T[0:group, :]

    row = lax.broadcasted_iota(jnp.int32, (LANES, LANES), 0)
    lane = lax.broadcasted_iota(jnp.int32, (LANES, LANES), 1)
    above = lane >= row
    nothing = jnp.zeros((LANES, LANES), F32)

    def build(channel, carry):
        rolled = []
        for tile in range(tap_count):
            values = jnp.broadcast_to(tap_tiles[tile, pl.ds(channel, 1), :], (LANES, LANES))
            rolled.append(pltpu.roll(values, 0, 1, stride=1, stride_axis=0))
        for tile in range(tap_count + 1):
            upper = rolled[tile] if tile < tap_count else nothing
            lower = rolled[tile - 1] if tile > 0 else nothing
            values = jnp.where(above, upper, lower)
            high = values.astype(BF16)
            low = (values - high.astype(F32)).astype(BF16)
            toeplitz[channel, 0:LANES, tile * LANES : (tile + 1) * LANES] = high
            toeplitz[channel, LANES : 2 * LANES, tile * LANES : (tile + 1) * LANES] = low
        return carry

    lax.fori_loop(0, group, build, 0)

    all_rows = blocks * group
    received(g_two, G_TWO)
    values = g_two[...].reshape(all_rows, width).astype(F32)
    for half in range(2):
        g_wide[half, 0:all_rows, :] = values[:, half * LANES : (half + 1) * LANES]
        g_wide[half, all_rows : all_rows + 2 * group, :] = jnp.zeros((2 * group, LANES), F32)

    def strided(channel, ahead=0):
        return pl.ds(channel + ahead * group, blocks, stride=group)

    def inputs_step(channel, carry):
        even = [g_wide[0, strided(channel, ahead), :].astype(BF16) for ahead in range(3)]
        odd = [g_wide[1, strided(channel, ahead), :].astype(BF16) for ahead in range(2)]
        top = jnp.concatenate([even[0], odd[0], even[1], odd[1]], axis=1)
        bottom = jnp.concatenate([odd[0], even[1], odd[1], even[2]], axis=1)
        both = jnp.concatenate([top, bottom], axis=0)
        g_cat[channel] = both
        result = contract(both, toeplitz[channel], 1, 1)
        result = result[:, 0:LANES] + result[:, LANES : 2 * LANES]
        gi_wide[0, strided(channel), :] = result[0:blocks]
        gi_wide[1, strided(channel), :] = result[blocks : 2 * blocks]
        return carry

    lax.fori_loop(0, group, inputs_step, 0)
    for half in range(2):
        gi_send[:, :, half * LANES : (half + 1) * LANES] = (
            gi_wide[half].astype(BF16).reshape(blocks, group, LANES)
        )
    to_far(gi_send, gi_two, GI_TWO)

    received(x_two, X_TWO)
    values = x_two[...].reshape(all_rows, width).astype(F32)
    for half in range(2):
        x_wide[half] = values[:, half * LANES : (half + 1) * LANES]
    keep = lane <= row

    def filter_step(channel, carry):
        both = jnp.concatenate(
            [x_wide[0, strided(channel), :], x_wide[1, strided(channel), :]], axis=0
        ).astype(BF16)
        product = contract(both, g_cat[channel], 0, 0)
        rolled = [
            pltpu.roll(product[:, tile * LANES : (tile + 1) * LANES], 1, 1, stride=1, stride_axis=0)
            for tile in range(tap_count + 1)
        ]
        for tile in range(tap_count):
            total = jnp.where(keep, rolled[tile], rolled[tile + 1])
            gf_tiles[tile, pl.ds(channel, 1), :] = jnp.sum(total, axis=0, keepdims=True)
        return carry

    lax.fori_loop(0, group, filter_step, 0)
    for tile in range(tap_count):
        gf_rows[tile * LANES : (tile + 1) * LANES, :] = gf_tiles[tile].T
    first_chunk = lax.broadcasted_iota(jnp.int32, (seqs, LANES), 1) < group
    for part in range(2):
        packed = jnp.zeros((seqs, LANES), F32)
        for lag in range(8 if part == 0 else lags - 8):
            rows = jnp.where(first_chunk, gf_rows[pl.ds(8 * part + lag, seqs, stride=lags), :], 0.0)
            packed = packed + (rows if lag == 0 else pltpu.roll(rows, 16 * lag, 1))
        gf_send[:, part, :] = packed

    def send_filter(step, carry):
        index = lax.rem(seq + step, seqs)
        remote(gf_send.at[index], gf_recv.at[column], GF, index, chan)
        return carry

    lax.fori_loop(1, seqs, send_filter, 0)
    local(gf_send.at[seq], gf_recv.at[column], GF)

    received(gi_two, GI_TWO)
    turned = contract(eye, gi_two[...].reshape(width, width), 1, 1)
    gi_turn[...] = turned.astype(BF16).reshape(gi_turn.shape)
    to_near(lambda index: gi_turn.at[index], columns_of(gi_out, near), GI_ONE)

    received(gf_recv, GF)
    for part in range(2):
        rows = gf_recv[:, part, :]
        count = 8 if part == 0 else lags - 8
        for tile in range(seqs // 8):
            values = swap_chunks(rows[8 * tile : 8 * tile + 8])
            gf_out[8 * part : 8 * part + count, tile * LANES : (tile + 1) * LANES] = values[0:count]

    received(gi_out, GI_ONE)
    for ref, which in (
        (g_one, G_ONE), (x_one, X_ONE), (tap_send, TAPS), (g_send, G_TWO), (x_send, X_TWO),
        (gi_send, GI_TWO), (gi_turn, GI_ONE), (gf_send, GF),
    ):
        sent(ref, which)


def per_device(inputs, grad_output, filter_taps, seqs, chans):
    rows, channels = inputs.shape
    lags = filter_taps.shape[0]
    nears = CORES * chans
    blocks = seqs // CORES
    width = channels // nears
    group = width // blocks
    total_lags = lags * seqs
    tiles = total_lags // LANES
    exchange = pltpu.VMEM((16, 16, width), BF16)
    return pl.pallas_call(
        kernel,
        out_shape=(
            jax.ShapeDtypeStruct(inputs.shape, BF16),
            jax.ShapeDtypeStruct(filter_taps.shape, F32),
        ),
        in_specs=[
            pl.BlockSpec(memory_space=pl.ANY),
            pl.BlockSpec(memory_space=pl.ANY),
            pl.BlockSpec(memory_space=pltpu.VMEM),
        ],
        out_specs=(
            pl.BlockSpec(memory_space=pl.ANY),
            pl.BlockSpec(memory_space=pltpu.VMEM),
        ),
        scratch_shapes=[
            exchange, exchange, exchange, exchange, exchange, exchange,
            pltpu.VMEM((seqs, 2, LANES), F32),
            pltpu.VMEM((seqs, 2, LANES), F32),
            pltpu.VMEM((total_lags, LANES), F32),
            pltpu.VMEM((tiles, group, LANES), F32),
            pltpu.VMEM((group, 2 * LANES, total_lags + LANES), BF16),
            pltpu.VMEM((2, (blocks + 2) * group, LANES), F32),
            pltpu.VMEM((2, blocks * group, LANES), F32),
            pltpu.VMEM((group, 2 * blocks, total_lags + LANES), BF16),
            pltpu.VMEM((2, blocks * group, LANES), F32),
            exchange, exchange, exchange,
            pltpu.VMEM((tiles, LANES, LANES), F32),
            pltpu.VMEM((total_lags, LANES), F32),
            pltpu.VMEM((seqs, 2, LANES), F32),
            pltpu.VMEM((seqs, 2, LANES), F32),
            pltpu.SemaphoreType.DMA((8,)),
            pltpu.SemaphoreType.DMA((8,)),
        ],
        compiler_params=pltpu.CompilerParams(
            collective_id=0, has_side_effects=True, vmem_limit_bytes=40 * 1024 * 1024
        ),
    )(inputs, grad_output, filter_taps)


def solution(mesh):
    return jax.shard_map(
        functools.partial(per_device, seqs=mesh.shape["seq"], chans=mesh.shape["chan"]),
        mesh=mesh,
        in_specs=(P(("seq", "chan"), None), P(("seq", "chan"), None), P("seq", "chan")),
        out_specs=(P(("seq", "chan"), None), P("seq", "chan")),
        check_vma=False,
    )
```

profile of v0, /device:TPU:1, one launch (start us, length us, event | category | flops | bytes accessed | tf_op | source)
XLA Modules:
  0.0 45.3 jit_solution(7327237373331410143)
XLA Ops:
  0.6 0.0 copy-start
  0.6 0.9 %copy-done = bf16[16,4096]{1,0:T(8,128)(2,1)S(1)} copy-done((bf16[16,4096]{1,0:T(8,128)(2,1)S(1)}, bf16[16,4096]{1,0:T(8,128)(2,1)}, u32[]{:S(2)}) %copy-start) | copy-done | bytes 131096
  1.5 0.0 copy-start.1
  1.5 0.9 %copy-done.1 = bf16[16,4096]{1,0:T(8,128)(2,1)S(1)} copy-done((bf16[16,4096]{1,0:T(8,128)(2,1)S(1)}, bf16[16,4096]{1,0:T(8,128)(2,1)}, u32[]{:S(2)}) %copy-start.1) | copy-done | bytes 131096
  2.4 0.0 copy-start.2
  2.4 0.8 %copy-done.2 = f32[12,512]{1,0:T(8,128)S(1)} copy-done((f32[12,512]{1,0:T(8,128)S(1)}, f32[12,512]{1,0:T(8,128)}, u32[]{:S(2)}) %copy-start.2) | copy-done | bytes 24600
  3.2 40.8 %shard_map.50 = (bf16[16,4096]{1,0:T(8,128)(2,1)S(1)}, f32[12,512]{1,0:T(8,128)S(1)}) custom-call(bf16[16,4096]{1,0:T(8,128)(2,1)S(1)} %copy-done, bf16[16,4096]{1,0:T(8,128)(2,1)S(1)} %copy-done.1, f32[12,512]{1,0:T(8,128)S(1)} %copy-done.2), custom_call_target="tpu_custom_call" | custom-call | tf_op jit(solution)/shard_map/pallas_call | solution.py:289
  44.0 0.7 %copy.7 = bf16[16,4096]{1,0:T(8,128)(2,1)} copy(bf16[16,4096]{1,0:T(8,128)(2,1)S(1)} %get-tuple-element.4) | data formatting | bytes 262144
  44.7 0.6 %copy.8 = f32[12,512]{1,0:T(8,128)} copy(f32[12,512]{1,0:T(8,128)S(1)} %get-tuple-element.5) | data formatting | bytes 49152
Async XLA Ops:
  0.6 0.9 %copy-start = (bf16[16,4096]{1,0:T(8,128)(2,1)S(1)}, bf16[16,4096]{1,0:T(8,128)(2,1)}, u32[]{:S(2)}) copy-start(bf16[16,4096]{1,0:T(8,128)(2,1)} %x_hbm.1) | copy-start | bytes 393220
  1.5 0.9 %copy-start.1 = (bf16[16,4096]{1,0:T(8,128)(2,1)S(1)}, bf16[16,4096]{1,0:T(8,128)(2,1)}, u32[]{:S(2)}) copy-start(bf16[16,4096]{1,0:T(8,128)(2,1)} %g_hbm.1) | copy-start | bytes 393220
  2.4 0.8 %copy-start.2 = (f32[12,512]{1,0:T(8,128)S(1)}, f32[12,512]{1,0:T(8,128)}, u32[]{:S(2)}) copy-start(f32[12,512]{1,0:T(8,128)} %taps_ref.1) | copy-start | bytes 73732
where the time goes:
time: 45.5 us; the launch traced here: 45.3 us
  Pallas kernels  40.8 us (90%)
  local copies, waits for them, and re-layouts  3.83 us (8%)
  between operations  0.65 us (1%)
    pallas_call x1, Pallas kernels, per_device(): pl.pallas_call(kernel, out_shape=(jax.ShapeDtypeStruct(inputs.shape, BF16...  40.8 us
    unnamed x8, local copies, waits for them, and re-layouts  3.83 us

commit v1 on v0

v1 whole, which is shorter than its diff:
```python
import functools

import jax
import jax.numpy as jnp
from jax import lax
from jax.experimental import pallas as pl
from jax.experimental.pallas import tpu as pltpu
from jax.sharding import PartitionSpec as P

MESH = pl.DeviceIdType.MESH
F32 = jnp.float32
BF16 = jnp.bfloat16
LANES = 128
HALF = LANES // 2
CORES = 2
ROW = 4
PLANES = 4
SHORT = 32
FOLDS = LANES // SHORT
UNROLL = 4

G_ONE, X_ONE, TAPS, G_TWO, X_TWO, HALO_FIRST, HALO_LAST, GI_TWO, GI_ONE, GF, TAPS_IN, GF_OUT = range(12)


def contract(lhs, rhs, lhs_dim, rhs_dim):
    return lax.dot_general(
        lhs, rhs, (((lhs_dim,), (rhs_dim,)), ((), ())), preferred_element_type=F32
    )


def left(values, by):
    return values if by % LANES == 0 else pltpu.roll(values, LANES - by % LANES, 1)


def kernel(
    x_hbm, g_hbm, taps_hbm, gi_out, gf_out,
    g_one, x_one, g_send, x_send, g_two, x_two,
    taps, tap_send, tap_recv, tap_rows, tap_tiles, toeplitz,
    g_wide, x_wide, g_cat, gi_wide, gi_send, gi_two, gi_turn,
    gf_partial, gf_rows, gf_send, gf_recv, gf_own,
    send_sem, recv_sem,
):
    seqs = lax.axis_size("seq")
    chans = lax.axis_size("chan")
    seq = lax.axis_index("seq")
    chan = lax.axis_index("chan")
    core = lax.rem(seq, CORES)
    block = lax.div(seq, CORES)
    plane = lax.div(block, ROW)
    place = lax.rem(block, ROW)
    near = core * chans + chan
    nears = CORES * chans
    columns = CORES * ROW
    column = core * ROW + place
    width = g_one.shape[2]
    lags = taps_hbm.shape[0]
    half_lags = lags // 2
    tap_count = tap_tiles.shape[0]
    group = tap_tiles.shape[1]
    rows_of_x = 2 * ROW

    def received(ref, which):
        pltpu.make_async_copy(ref, ref, recv_sem.at[which]).wait()

    def sent(ref, which):
        pltpu.make_async_copy(ref, ref, send_sem.at[which]).wait()

    def remote(src, dst, which, to_seq, to_chan):
        pltpu.make_async_remote_copy(
            src_ref=src, dst_ref=dst, send_sem=send_sem.at[which], recv_sem=recv_sem.at[which],
            device_id={"seq": to_seq, "chan": to_chan}, device_id_type=MESH,
        ).start()

    def local(src, dst, which):
        pltpu.make_async_copy(src, dst, recv_sem.at[which]).start()

    with jax.named_scope("greet"):
        local(taps_hbm, taps, TAPS_IN)
        barrier = pltpu.get_barrier_semaphore()

        def greet_seq(step, carry):
            pl.semaphore_signal(
                barrier, inc=1, device_id={"seq": lax.rem(seq + step, seqs), "chan": chan}, device_id_type=MESH
            )
            return carry

        def greet_near(step, carry):
            other = lax.rem(chan + step, chans)
            for other_core in range(CORES):
                pl.semaphore_signal(
                    barrier, inc=1, device_id={"seq": block * CORES + other_core, "chan": other}, device_id_type=MESH
                )
            return carry

        lax.fori_loop(1, seqs, greet_seq, 0)
        lax.fori_loop(1, chans, greet_near, 0)

    first_half = lax.broadcasted_iota(jnp.int32, (8, LANES), 1) < HALF

    with jax.named_scope("pack_taps"):
        received(taps, TAPS_IN)
        nothing = jnp.zeros((8 - half_lags, LANES), F32)
        for tile in range(columns // 2):
            lanes = slice(tile * LANES, (tile + 1) * LANES)
            early = jnp.concatenate([taps[0:half_lags, lanes], nothing], axis=0)
            late = jnp.concatenate([taps[half_lags:lags, lanes], nothing], axis=0)
            tap_send[2 * tile] = jnp.where(first_half, early, left(late, HALF))
            tap_send[2 * tile + 1] = jnp.where(first_half, left(early, HALF), late)

    row = lax.broadcasted_iota(jnp.int32, (width, width), 0)
    lane = lax.broadcasted_iota(jnp.int32, (width, width), 1)
    eye = (row == lane).astype(F32).astype(BF16)
    flip = ((row ^ lane) == LANES - 1).astype(F32).astype(BF16)

    with jax.named_scope("barrier"):
        pl.semaphore_wait(barrier, seqs - 1 + CORES * (chans - 1))

    def columns_of(ref, index):
        other_core = lax.div(index, chans)
        other_chan = lax.rem(index, chans)
        start = pl.multiple_of(other_chan * (CORES * width) + other_core * width, width)
        return ref.at[:, pl.ds(start, width)]

    def to_near(src_of, dst, which):
        def step(shift, carry):
            index = lax.rem(near + shift, nears)
            remote(src_of(index), dst, which, block * CORES + lax.div(index, chans), lax.rem(index, chans))
            return carry

        lax.fori_loop(1, nears, step, 0)
        local(src_of(near), dst, which)

    def to_row(src, dst, which):
        for shift in range(1, ROW):
            index = lax.rem(place + shift, ROW)
            remote(src.at[index], dst.at[place], which, (plane * ROW + index) * CORES + core, chan)
        local(src.at[place], dst.at[place], which)

    def to_seq(src_of, dst, which):
        def step(shift, carry):
            index = lax.rem(seq + shift, seqs)
            remote(src_of(index), dst, which, index, chan)
            return carry

        lax.fori_loop(1, seqs, step, 0)
        local(src_of(seq), dst, which)

    def column_of(index):
        return lax.rem(index, CORES) * ROW + lax.rem(lax.div(index, CORES), ROW)

    with jax.named_scope("send_one"):
        to_near(functools.partial(columns_of, g_hbm), g_one.at[near], G_ONE)
        to_seq(lambda index: tap_send.at[column_of(index)], tap_recv.at[seq], TAPS)
        to_near(functools.partial(columns_of, x_hbm), x_one.at[near], X_ONE)

    with jax.named_scope("turn_g"):
        received(g_one, G_ONE)
        turned = contract(eye, g_one[...].reshape(width, width), 1, 1)
        g_send[...] = turned.astype(BF16).reshape(g_send.shape)

    with jax.named_scope("send_g_two"):
        to_row(g_send, g_two, G_TWO)

        def send_halo(src, dst, which):
            for index in range(ROW):
                remote(src.at[index], dst, which, ((plane - 1) * ROW + index) * CORES + core, chan)

        @pl.when((plane > 0) & (place == 0))
        def _():
            send_halo(g_send, g_two.at[ROW], HALO_FIRST)

        @pl.when((plane > 0) & (place == 1))
        def _():
            send_halo(g_send.at[:, :, 0:LANES], g_two.at[ROW + 1, :, 0:LANES], HALO_LAST)

    with jax.named_scope("turn_x"):
        received(x_one, X_ONE)
        turned = contract(eye, x_one[...].reshape(width, width), 1, 1).astype(BF16)
        turned = contract(turned, flip, 1, 0)
        x_send[...] = turned.astype(BF16).reshape(x_send.shape)
        to_row(x_send, x_two, X_TWO)

    with jax.named_scope("unpack_taps"):
        received(tap_recv, TAPS)
        for lag in range(half_lags):
            rows = tap_recv[:, lag, :]
            tap_rows[pl.ds(lag, seqs, stride=lags), :] = rows
            tap_rows[pl.ds(half_lags + lag, seqs, stride=lags), :] = left(rows, HALF)
        for tile in range(tap_count):
            tap_tiles[tile] = tap_rows[tile * LANES : (tile + 1) * LANES, :].T[0:group, :]

    row = lax.broadcasted_iota(jnp.int32, (SHORT, LANES), 0)
    lane = lax.broadcasted_iota(jnp.int32, (SHORT, LANES), 1)
    ahead = lane >= row
    nothing = jnp.zeros((SHORT, LANES), F32)

    def build(channel):
        rolled = []
        for tile in range(tap_count):
            values = jnp.broadcast_to(tap_tiles[tile, pl.ds(channel, 1), :], (SHORT, LANES))
            rolled.append(pltpu.roll(values, 0, 1, stride=1, stride_axis=0))
        for tile in range(tap_count + 1):
            upper = rolled[tile] if tile < tap_count else nothing
            lower = rolled[tile - 1] if tile > 0 else nothing
            values = jnp.where(ahead, upper, lower)
            high = values.astype(BF16)
            low = (values - high.astype(F32)).astype(BF16)
            toeplitz[channel, 0:SHORT, tile * LANES : (tile + 1) * LANES] = high
            toeplitz[channel, SHORT : 2 * SHORT, tile * LANES : (tile + 1) * LANES] = low

    def for_channels(body):
        def step(first, carry):
            for extra in range(UNROLL):
                body(first * UNROLL + extra)
            return carry

        lax.fori_loop(0, group // UNROLL, step, 0)

    with jax.named_scope("toeplitz"):
        for_channels(build)

    def widen(source, target, slots):
        for slot in slots:
            for half in range(2):
                start = (2 * slot + half) * group
                target[start : start + group, :] = source[slot, :, half * LANES : (half + 1) * LANES].astype(F32)

    with jax.named_scope("widen_g"):
        received(g_two.at[pl.ds(0, ROW)], G_TWO)
        widen(g_two, g_wide, range(ROW))

        @pl.when(plane < PLANES - 1)
        def _():
            received(g_two.at[ROW], HALO_FIRST)
            received(g_two.at[ROW + 1, :, 0:LANES], HALO_LAST)
            widen(g_two, g_wide, (ROW,))
            g_wide[(rows_of_x + 2) * group : (rows_of_x + 3) * group, :] = g_two[ROW + 1, :, 0:LANES].astype(F32)

        @pl.when(plane == PLANES - 1)
        def _():
            g_wide[rows_of_x * group : (rows_of_x + 3) * group, :] = jnp.zeros((3 * group, LANES), F32)

    with jax.named_scope("widen_x"):
        received(x_two, X_TWO)
        widen(x_two, x_wide, range(ROW))

    def strided(channel, blocks_ahead=0):
        return pl.ds(channel + blocks_ahead * group, rows_of_x, stride=group)

    lane_of_row = lax.broadcasted_iota(jnp.int32, (rows_of_x, LANES), 1)
    keep = lane - row < LANES - SHORT + 1

    def filter_step(channel):
        blocks = [g_wide[strided(channel, tile), :] for tile in range(tap_count + 1)]
        folds = []
        for fold in range(FOLDS):
            shifted = [left(values, SHORT * fold) for values in blocks]
            if fold > 0:
                near_end = lane_of_row < LANES - SHORT * fold
                shifted = [
                    jnp.where(near_end, shifted[tile], shifted[tile + 1]) for tile in range(tap_count)
                ] + [shifted[tap_count]]
            folds.append(jnp.concatenate(shifted, axis=1))
        windows = jnp.concatenate(folds, axis=0).astype(BF16)
        g_cat[channel] = windows
        source = x_wide[strided(channel), :]
        mine = jnp.concatenate(
            [left(source, LANES - SHORT * (fold + 1)) for fold in range(FOLDS)], axis=0
        ).astype(BF16)
        product = contract(mine[:, 0:SHORT], windows, 0, 0)
        rolled = [
            pltpu.roll(
                product[:, tile * LANES : (tile + 1) * LANES], LANES - SHORT + 1, 1, stride=1, stride_axis=0
            )
            for tile in range(tap_count + 1)
        ]
        for tile in range(tap_count):
            total = jnp.where(keep, rolled[tile], rolled[tile + 1])
            total = (total[0:8] + total[8:16]) + (total[16:24] + total[24:32])
            gf_partial[tile, pl.ds(pl.multiple_of(channel * 8, 8), 8), :] = total

    with jax.named_scope("grad_filter"):
        for_channels(filter_step)

    with jax.named_scope("send_gf"):
        for tile in range(tap_count):
            total = gf_partial[tile, pl.ds(0, group, stride=8), :]
            for part in range(1, 8):
                total = total + gf_partial[tile, pl.ds(part, group, stride=8), :]
            total = jnp.concatenate([total, jnp.zeros((LANES - group, LANES), F32)], axis=0)
            gf_rows[tile * LANES : (tile + 1) * LANES, :] = total.T
        for lag in range(half_lags):
            early = gf_rows[pl.ds(lag, seqs, stride=lags), :]
            late = gf_rows[pl.ds(half_lags + lag, seqs, stride=lags), :]
            gf_send[:, lag, :] = early + left(late, HALF)
        for lag in range(half_lags, 8):
            gf_send[:, lag, :] = jnp.zeros((seqs, LANES), F32)
        to_seq(lambda index: gf_send.at[index], gf_recv.at[plane * columns + column], GF)

    def inputs_step(channel):
        result = contract(g_cat[channel], toeplitz[channel], 1, 1)
        result = jnp.concatenate([result, jnp.zeros((SHORT, LANES - 2 * SHORT), F32)], axis=1)
        result = result + left(result, SHORT)
        total = result[0:rows_of_x]
        for fold in range(1, FOLDS):
            part = pltpu.roll(result[fold * rows_of_x : (fold + 1) * rows_of_x], SHORT * fold, 1)
            total = jnp.where(lane_of_row < SHORT * fold, total, part)
        gi_wide[strided(channel), :] = total

    with jax.named_scope("grad_inputs"):
        for_channels(inputs_step)

    with jax.named_scope("send_gi_two"):
        for slot in range(ROW):
            for half in range(2):
                start = (2 * slot + half) * group
                gi_send[slot, :, half * LANES : (half + 1) * LANES] = gi_wide[start : start + group, :].astype(BF16)
        to_row(gi_send, gi_two, GI_TWO)

    with jax.named_scope("turn_gi"):
        received(gi_two, GI_TWO)
        turned = contract(eye, gi_two[...].reshape(width, width), 1, 1)
        gi_turn[...] = turned.astype(BF16).reshape(gi_turn.shape)
        to_near(lambda index: gi_turn.at[index], columns_of(gi_out, near), GI_ONE)

    with jax.named_scope("unpack_gf"):
        received(gf_recv, GF)
        sums = []
        for index in range(columns):
            total = gf_recv[index]
            for other in range(1, PLANES):
                total = total + gf_recv[other * columns + index]
            sums.append(total)
        for tile in range(columns // 2):
            lanes = slice(tile * LANES, (tile + 1) * LANES)
            early = jnp.where(first_half, sums[2 * tile], left(sums[2 * tile + 1], HALF))
            late = jnp.where(first_half, left(sums[2 * tile], HALF), sums[2 * tile + 1])
            gf_own[0:half_lags, lanes] = early[0:half_lags]
            gf_own[half_lags:lags, lanes] = late[0:half_lags]
        local(gf_own, gf_out, GF_OUT)

    with jax.named_scope("finish"):
        for ref, which in (
            (g_one, G_ONE), (x_one, X_ONE), (tap_recv, TAPS), (g_send, G_TWO), (x_send, X_TWO),
            (gi_send, GI_TWO), (gi_turn, GI_ONE), (gf_send, GF),
        ):
            sent(ref.at[pl.ds(0, ref.shape[0] - 1)], which)

        @pl.when((plane > 0) & (place == 0))
        def _():
            sent(g_send, HALO_FIRST)

        @pl.when((plane > 0) & (place == 1))
        def _():
            sent(g_send.at[:, :, 0:LANES], HALO_LAST)

        received(gf_out, GF_OUT)
        received(gi_out, GI_ONE)


def per_device(inputs, grad_output, filter_taps, seqs, chans):
    rows, channels = inputs.shape
    lags, tap_channels = filter_taps.shape
    nears = CORES * chans
    width = channels // nears
    group = width // ROW
    columns = CORES * ROW
    total_lags = lags * seqs
    tiles = total_lags // LANES
    window = total_lags + LANES
    one = pltpu.VMEM((nears, rows, width), BF16)
    two = pltpu.VMEM((ROW, group, width), BF16)
    return pl.pallas_call(
        kernel,
        out_shape=(
            jax.ShapeDtypeStruct(inputs.shape, BF16),
            jax.ShapeDtypeStruct(filter_taps.shape, F32),
        ),
        in_specs=[pl.BlockSpec(memory_space=pl.ANY)] * 3,
        out_specs=(pl.BlockSpec(memory_space=pl.ANY), pl.BlockSpec(memory_space=pl.ANY)),
        scratch_shapes=[
            one, one, two, two,
            pltpu.VMEM((ROW + 2, group, width), BF16),
            two,
            pltpu.VMEM(filter_taps.shape, F32),
            pltpu.VMEM((columns, 8, LANES), F32),
            pltpu.VMEM((seqs, 8, LANES), F32),
            pltpu.VMEM((total_lags, LANES), F32),
            pltpu.VMEM((tiles, group, LANES), F32),
            pltpu.VMEM((group, 2 * SHORT, window), BF16),
            pltpu.VMEM(((2 * ROW + 3) * group, LANES), F32),
            pltpu.VMEM((2 * ROW * group, LANES), F32),
            pltpu.VMEM((group, SHORT, window), BF16),
            pltpu.VMEM((2 * ROW * group, LANES), F32),
            two, two, one,
            pltpu.VMEM((tiles, group * 8, LANES), F32),
            pltpu.VMEM((total_lags, LANES), F32),
            pltpu.VMEM((seqs, 8, LANES), F32),
            pltpu.VMEM((seqs, 8, LANES), F32),
            pltpu.VMEM(filter_taps.shape, F32),
            pltpu.SemaphoreType.DMA((12,)),
            pltpu.SemaphoreType.DMA((12,)),
        ],
        compiler_params=pltpu.CompilerParams(
            collective_id=0, has_side_effects=True, vmem_limit_bytes=48 * 1024 * 1024
        ),
    )(inputs, grad_output, filter_taps)


def solution(mesh):
    return jax.shard_map(
        functools.partial(per_device, seqs=mesh.shape["seq"], chans=mesh.shape["chan"]),
        mesh=mesh,
        in_specs=(P(("seq", "chan"), None), P(("seq", "chan"), None), P("seq", "chan")),
        out_specs=(P(("seq", "chan"), None), P("seq", "chan")),
        check_vma=False,
    )
```

time: 45.5 us -> 53.1 us (1.17)
  Pallas kernels: 40.8 us -> 48.4 us
    pallas_call x1, Pallas kernels: 40.8 us -> 48.4 us  [per_device(): pl.pallas_call(kernel, out_shape=(jax.ShapeDtypeStruct(inputs.shape, BF16...]
where the time goes in v1:
time: 53.1 us; the launch traced here: 52.9 us
  Pallas kernels  48.4 us (91%)
  local copies, waits for them, and re-layouts  3.83 us (7%)
  between operations  0.65 us (1%)
    pallas_call x1, Pallas kernels, per_device(): pl.pallas_call(kernel, out_shape=(jax.ShapeDtypeStruct(inputs.shape, BF16...  48.4 us
    unnamed x8, local copies, waits for them, and re-layouts  3.83 us

profile of v1, /device:TPU:1, one launch (start us, length us, event | category | flops | bytes accessed | tf_op | source)
XLA Modules:
  0.0 52.9 jit_solution(15440596297649943753)
XLA Ops:
  0.6 0.0 copy-start
  0.6 0.9 %copy-done = bf16[16,4096]{1,0:T(8,128)(2,1)S(1)} copy-done((bf16[16,4096]{1,0:T(8,128)(2,1)S(1)}, bf16[16,4096]{1,0:T(8,128)(2,1)}, u32[]{:S(2)}) %copy-start) | copy-done | bytes 131096
  1.5 0.0 copy-start.1
  1.5 0.9 %copy-done.1 = bf16[16,4096]{1,0:T(8,128)(2,1)S(1)} copy-done((bf16[16,4096]{1,0:T(8,128)(2,1)S(1)}, bf16[16,4096]{1,0:T(8,128)(2,1)}, u32[]{:S(2)}) %copy-start.1) | copy-done | bytes 131096
  2.4 0.0 copy-start.2
  2.4 0.8 %copy-done.2 = f32[12,512]{1,0:T(8,128)S(1)} copy-done((f32[12,512]{1,0:T(8,128)S(1)}, f32[12,512]{1,0:T(8,128)}, u32[]{:S(2)}) %copy-start.2) | copy-done | bytes 24600
  3.2 48.4 %shard_map.50 = (bf16[16,4096]{1,0:T(8,128)(2,1)S(1)}, f32[12,512]{1,0:T(8,128)S(1)}) custom-call(bf16[16,4096]{1,0:T(8,128)(2,1)S(1)} %copy-done, bf16[16,4096]{1,0:T(8,128)(2,1)S(1)} %copy-done.1, f32[12,512]{1,0:T(8,128)S(1)} %copy-done.2), custom_call_target="tpu_custom_call" | custom-call | tf_op jit(solution)/shard_map/pallas_call | solution.py:373
  51.6 0.7 %copy.7 = bf16[16,4096]{1,0:T(8,128)(2,1)} copy(bf16[16,4096]{1,0:T(8,128)(2,1)S(1)} %get-tuple-element.4) | data formatting | bytes 262144
  52.3 0.6 %copy.8 = f32[12,512]{1,0:T(8,128)} copy(f32[12,512]{1,0:T(8,128)S(1)} %get-tuple-element.5) | data formatting | bytes 49152
Async XLA Ops:
  0.6 0.9 %copy-start = (bf16[16,4096]{1,0:T(8,128)(2,1)S(1)}, bf16[16,4096]{1,0:T(8,128)(2,1)}, u32[]{:S(2)}) copy-start(bf16[16,4096]{1,0:T(8,128)(2,1)} %x_hbm.1) | copy-start | bytes 393220
  1.5 0.9 %copy-start.1 = (bf16[16,4096]{1,0:T(8,128)(2,1)S(1)}, bf16[16,4096]{1,0:T(8,128)(2,1)}, u32[]{:S(2)}) copy-start(bf16[16,4096]{1,0:T(8,128)(2,1)} %g_hbm.1) | copy-start | bytes 393220
  2.4 0.8 %copy-start.2 = (f32[12,512]{1,0:T(8,128)S(1)}, f32[12,512]{1,0:T(8,128)}, u32[]{:S(2)}) copy-start(f32[12,512]{1,0:T(8,128)} %taps_hbm.1) | copy-start | bytes 73732

commit v2 on v1

v2 whole, which is shorter than its diff:
```python
import functools

import jax
import jax.numpy as jnp
from jax import lax
from jax.experimental import pallas as pl
from jax.experimental.pallas import tpu as pltpu
from jax.sharding import PartitionSpec as P

MESH = pl.DeviceIdType.MESH
F32 = jnp.float32
BF16 = jnp.bfloat16
LANES = 128
HALF = LANES // 2
CORES = 2
ROW = 4
PLANES = 4
SHORT = 32
FOLDS = LANES // SHORT

G_ONE, X_ONE, TAPS, G_TWO, X_TWO, HALO_EVEN, HALO_ODD, GI_TWO, GI_ONE, GF, TAPS_IN, GF_OUT = range(12)


def contract(lhs, rhs, lhs_dim, rhs_dim):
    return lax.dot_general(
        lhs, rhs, (((lhs_dim,), (rhs_dim,)), ((), ())), preferred_element_type=F32
    )


def left(values, by):
    return values if by % LANES == 0 else pltpu.roll(values, LANES - by % LANES, 1)


def kernel(
    x_hbm, g_hbm, taps_hbm, gi_out, gf_out,
    g_one, x_one, g_send, x_send, g_two, g_halo, x_two,
    taps, tap_send, tap_recv, tap_rows, tap_tiles, toeplitz,
    g_wide, x_wide, g_cat, gi_wide, gi_send, gi_two, gi_turn,
    gf_partial, gf_rows, gf_send, gf_recv, gf_own,
    send_sem, recv_sem,
):
    seqs = lax.axis_size("seq")
    chans = lax.axis_size("chan")
    seq = lax.axis_index("seq")
    chan = lax.axis_index("chan")
    core = lax.rem(seq, CORES)
    block = lax.div(seq, CORES)
    plane = lax.div(block, ROW)
    place = lax.rem(block, ROW)
    sibling = 1 - core
    slots = ROW * chans
    slot = place * chans + chan
    columns = CORES * ROW
    lags = taps_hbm.shape[0]
    half_lags = lags // 2
    tap_count = tap_tiles.shape[0]
    group = tap_tiles.shape[1]
    rows_of_x = CORES * ROW

    def received(ref, which):
        pltpu.make_async_copy(ref, ref, recv_sem.at[which]).wait()

    def sent(ref, which):
        pltpu.make_async_copy(ref, ref, send_sem.at[which]).wait()

    def remote(src, dst, which, to_seq, to_chan):
        pltpu.make_async_remote_copy(
            src_ref=src, dst_ref=dst, send_sem=send_sem.at[which], recv_sem=recv_sem.at[which],
            device_id={"seq": to_seq, "chan": to_chan}, device_id_type=MESH,
        ).start()

    def local(src, dst, which):
        pltpu.make_async_copy(src, dst, recv_sem.at[which]).start()

    with jax.named_scope("greet"):
        local(taps_hbm, taps, TAPS_IN)
        barrier = pltpu.get_barrier_semaphore()

        def greet_seq(step, carry):
            pl.semaphore_signal(
                barrier, inc=1, device_id={"seq": lax.rem(seq + step, seqs), "chan": chan}, device_id_type=MESH
            )
            return carry

        def greet_plane(step, carry):
            other = lax.rem(chan + step, chans)
            for index in range(ROW):
                pl.semaphore_signal(
                    barrier,
                    inc=1,
                    device_id={"seq": (plane * ROW + index) * CORES + core, "chan": other},
                    device_id_type=MESH,
                )
            return carry

        lax.fori_loop(1, seqs, greet_seq, 0)
        lax.fori_loop(1, chans, greet_plane, 0)

    first_half = lax.broadcasted_iota(jnp.int32, (8, LANES), 1) < HALF

    with jax.named_scope("pack_taps"):
        received(taps, TAPS_IN)
        nothing = jnp.zeros((8 - half_lags, LANES), F32)
        for tile in range(columns // 2):
            lanes = slice(tile * LANES, (tile + 1) * LANES)
            early = jnp.concatenate([taps[0:half_lags, lanes], nothing], axis=0)
            late = jnp.concatenate([taps[half_lags:lags, lanes], nothing], axis=0)
            tap_send[2 * tile] = jnp.where(first_half, early, left(late, HALF))
            tap_send[2 * tile + 1] = jnp.where(first_half, left(early, HALF), late)

    row = lax.broadcasted_iota(jnp.int32, (LANES, LANES), 0)
    lane = lax.broadcasted_iota(jnp.int32, (LANES, LANES), 1)
    eye = (row == lane).astype(F32).astype(BF16)
    flip = (row + lane == LANES - 1).astype(F32).astype(BF16)

    with jax.named_scope("barrier"):
        pl.semaphore_wait(barrier, seqs - 1 + ROW * (chans - 1))

    def columns_of(ref, index):
        start = lax.rem(index, chans) * (ROW * LANES) + lax.div(index, chans) * LANES
        return ref.at[:, pl.ds(pl.multiple_of(start, LANES), LANES)]

    def to_plane(src_of, dst, which):
        def step(shift, carry):
            index = slot + shift
            index = jnp.where(index >= slots, index - slots, index)
            to = (plane * ROW + lax.div(index, chans)) * CORES + core
            remote(src_of(index), dst, which, to, lax.rem(index, chans))
            return carry

        lax.fori_loop(1, slots, step, 0)
        local(src_of(slot), dst, which)

    def to_sibling(src, dst, which):
        remote(src.at[sibling], dst.at[core], which, block * CORES + sibling, chan)
        local(src.at[core], dst.at[core], which)

    def to_seq(src_of, dst, which):
        def step(shift, carry):
            index = seq + shift
            index = jnp.where(index >= seqs, index - seqs, index)
            remote(src_of(index), dst, which, index, chan)
            return carry

        lax.fori_loop(1, seqs, step, 0)
        local(src_of(seq), dst, which)

    with jax.named_scope("send_one"):
        to_plane(functools.partial(columns_of, g_hbm), g_one.at[slot], G_ONE)
        to_seq(lambda index: tap_send.at[lax.rem(index, columns)], tap_recv.at[seq], TAPS)
        to_plane(functools.partial(columns_of, x_hbm), x_one.at[slot], X_ONE)

    def turn(source, index):
        rows = source[chans * index : chans * (index + 1)].reshape(LANES, LANES)
        return contract(eye, rows, 1, 1).astype(BF16)

    def by_core(rows):
        return rows.reshape(CORES, group, LANES)

    with jax.named_scope("turn_g"):
        received(g_one, G_ONE)
        for index in range(ROW):
            g_send[:, :, index * LANES : (index + 1) * LANES] = by_core(turn(g_one, index))

    with jax.named_scope("send_g_two"):
        to_sibling(g_send, g_two, G_TWO)

        def send_halo(width, which):
            for to_core in range(CORES):
                remote(
                    g_send.at[to_core, :, 0:width], g_halo.at[core, :, 0:width], which,
                    ((plane - 1) * ROW + place) * CORES + to_core, chan,
                )

        @pl.when((plane > 0) & (core == 0))
        def _():
            send_halo(2 * LANES, HALO_EVEN)

        @pl.when((plane > 0) & (core == 1))
        def _():
            send_halo(LANES, HALO_ODD)

    with jax.named_scope("turn_x"):
        received(x_one, X_ONE)
        for index in range(ROW):
            turned = contract(turn(x_one, index), flip, 1, 0).astype(BF16)
            x_send[:, :, index * LANES : (index + 1) * LANES] = by_core(turned)
        to_sibling(x_send, x_two, X_TWO)

    with jax.named_scope("unpack_taps"):
        received(tap_recv, TAPS)
        for lag in range(half_lags):
            rows = tap_recv[:, lag, :]
            tap_rows[pl.ds(lag, seqs, stride=lags), :] = rows
            tap_rows[pl.ds(half_lags + lag, seqs, stride=lags), :] = left(rows, HALF)
        for tile in range(tap_count):
            tap_tiles[tile] = tap_rows[tile * LANES : (tile + 1) * LANES, :].T[0:group, :]

    row = lax.broadcasted_iota(jnp.int32, (SHORT, LANES), 0)
    lane = lax.broadcasted_iota(jnp.int32, (SHORT, LANES), 1)
    ahead = lane >= row
    nothing = jnp.zeros((SHORT, LANES), F32)

    def build(channel):
        rolled = []
        for tile in range(tap_count):
            values = jnp.broadcast_to(tap_tiles[tile, pl.ds(channel, 1), :], (SHORT, LANES))
            rolled.append(pltpu.roll(values, 0, 1, stride=1, stride_axis=0))
        for tile in range(tap_count + 1):
            upper = rolled[tile] if tile < tap_count else nothing
            lower = rolled[tile - 1] if tile > 0 else nothing
            values = jnp.where(ahead, upper, lower)
            high = values.astype(BF16)
            low = (values - high.astype(F32)).astype(BF16)
            toeplitz[channel, 0:SHORT, tile * LANES : (tile + 1) * LANES] = high
            toeplitz[channel, SHORT : 2 * SHORT, tile * LANES : (tile + 1) * LANES] = low

    def for_channels(body, unroll):
        def step(first, carry):
            for extra in range(unroll):
                body(first * unroll + extra)
            return carry

        lax.fori_loop(0, group // unroll, step, 0)

    with jax.named_scope("toeplitz"):
        for_channels(build, 16)

    def widen(source, target, index, from_core, at):
        target[at * group : (at + 1) * group, :] = source[
            from_core, :, index * LANES : (index + 1) * LANES
        ].astype(F32)

    with jax.named_scope("widen_g"):
        received(g_two, G_TWO)
        for index in range(ROW):
            for from_core in range(CORES):
                widen(g_two, g_wide, index, from_core, CORES * index + from_core)

        @pl.when(plane < PLANES - 1)
        def _():
            received(g_halo.at[0], HALO_EVEN)
            received(g_halo.at[1, :, 0:LANES], HALO_ODD)
            widen(g_halo, g_wide, 0, 0, rows_of_x)
            widen(g_halo, g_wide, 0, 1, rows_of_x + 1)
            widen(g_halo, g_wide, 1, 0, rows_of_x + 2)

        @pl.when(plane == PLANES - 1)
        def _():
            g_wide[rows_of_x * group : (rows_of_x + 3) * group, :] = jnp.zeros((3 * group, LANES), F32)

    def strided(channel, blocks_ahead=0):
        return pl.ds(channel + blocks_ahead * group, rows_of_x, stride=group)

    lane_of_row = lax.broadcasted_iota(jnp.int32, (rows_of_x, LANES), 1)
    keep = lane - row < LANES - SHORT + 1

    def window_step(channel):
        blocks = [g_wide[strided(channel, tile), :] for tile in range(tap_count + 1)]
        folds = []
        for fold in range(FOLDS):
            shifted = [left(values, SHORT * fold) for values in blocks]
            if fold > 0:
                near_end = lane_of_row < LANES - SHORT * fold
                shifted = [
                    jnp.where(near_end, shifted[tile], shifted[tile + 1]) for tile in range(tap_count)
                ] + [shifted[tap_count]]
            folds.append(jnp.concatenate(shifted, axis=1))
        g_cat[channel] = jnp.concatenate(folds, axis=0).astype(BF16)

    with jax.named_scope("windows"):
        for_channels(window_step, 16)

    def filter_step(channel):
        source = x_wide[strided(channel), :]
        mine = jnp.concatenate(
            [left(source, LANES - SHORT * (fold + 1)) for fold in range(FOLDS)], axis=0
        ).astype(BF16)
        product = contract(mine[:, 0:SHORT], g_cat[channel], 0, 0)
        rolled = [
            pltpu.roll(
                product[:, tile * LANES : (tile + 1) * LANES], LANES - SHORT + 1, 1, stride=1, stride_axis=0
            )
            for tile in range(tap_count + 1)
        ]
        for tile in range(tap_count):
            total = jnp.where(keep, rolled[tile], rolled[tile + 1])
            total = (total[0:8] + total[8:16]) + (total[16:24] + total[24:32])
            gf_partial[tile, pl.ds(pl.multiple_of(channel * 8, 8), 8), :] = total

    def inputs_step(channel):
        result = contract(g_cat[channel], toeplitz[channel], 1, 1)
        result = jnp.concatenate([result, jnp.zeros((SHORT, LANES - 2 * SHORT), F32)], axis=1)
        result = result + left(result, SHORT)
        total = result[0:rows_of_x]
        for fold in range(1, FOLDS):
            part = pltpu.roll(result[fold * rows_of_x : (fold + 1) * rows_of_x], SHORT * fold, 1)
            total = jnp.where(lane_of_row < SHORT * fold, total, part)
        gi_wide[strided(channel), :] = total

    filter_first = plane >= PLANES // 2
    filter_turn = jnp.where(filter_first, 0, 1)

    def two_turns(index, carry):
        @pl.when(index == filter_turn)
        def _():
            received(x_two, X_TWO)
            for place_from in range(ROW):
                for from_core in range(CORES):
                    widen(x_two, x_wide, place_from, from_core, CORES * place_from + from_core)
            for_channels(filter_step, 8)
            for tile in range(tap_count):
                total = gf_partial[tile, pl.ds(0, group, stride=8), :]
                for part in range(1, 8):
                    total = total + gf_partial[tile, pl.ds(part, group, stride=8), :]
                total = jnp.concatenate([total, jnp.zeros((LANES - group, LANES), F32)], axis=0)
                gf_rows[tile * LANES : (tile + 1) * LANES, :] = total.T
            for lag in range(half_lags):
                early = gf_rows[pl.ds(lag, seqs, stride=lags), :]
                late = gf_rows[pl.ds(half_lags + lag, seqs, stride=lags), :]
                gf_send[:, lag, :] = early + left(late, HALF)
            for lag in range(half_lags, 8):
                gf_send[:, lag, :] = jnp.zeros((seqs, LANES), F32)
            to_seq(lambda to: gf_send.at[to], gf_recv.at[seq], GF)

        @pl.when(index != filter_turn)
        def _():
            for_channels(inputs_step, 16)
            for place_to in range(ROW):
                for to_core in range(CORES):
                    start = (CORES * place_to + to_core) * group
                    gi_send[to_core, :, place_to * LANES : (place_to + 1) * LANES] = gi_wide[
                        start : start + group, :
                    ].astype(BF16)
            to_sibling(gi_send, gi_two, GI_TWO)

        return carry

    with jax.named_scope("both_gradients"):
        lax.fori_loop(0, 2, two_turns, 0)

    with jax.named_scope("turn_gi"):
        received(gi_two, GI_TWO)
        for index in range(ROW):
            rows = gi_two[:, :, index * LANES : (index + 1) * LANES].reshape(LANES, LANES)
            turned = contract(eye, rows, 1, 1).astype(BF16)
            gi_turn[chans * index : chans * (index + 1)] = turned.reshape(chans, LANES // chans, LANES)
        to_plane(lambda index: gi_turn.at[index], columns_of(gi_out, slot), GI_ONE)

    with jax.named_scope("unpack_gf"):
        received(gf_recv, GF)
        sums = []
        for index in range(columns):
            total = gf_recv[index]
            for other in range(1, PLANES):
                total = total + gf_recv[other * columns + index]
            sums.append(total)
        for tile in range(columns // 2):
            lanes = slice(tile * LANES, (tile + 1) * LANES)
            early = jnp.where(first_half, sums[2 * tile], left(sums[2 * tile + 1], HALF))
            late = jnp.where(first_half, left(sums[2 * tile], HALF), sums[2 * tile + 1])
            gf_own[0:half_lags, lanes] = early[0:half_lags]
            gf_own[half_lags:lags, lanes] = late[0:half_lags]
        local(gf_own, gf_out, GF_OUT)

    with jax.named_scope("finish"):
        for ref, which in (
            (g_one, G_ONE), (x_one, X_ONE), (tap_recv, TAPS), (g_send, G_TWO), (x_send, X_TWO),
            (gi_send, GI_TWO), (gi_turn, GI_ONE), (gf_send, GF),
        ):
            sent(ref.at[pl.ds(0, ref.shape[0] - 1)], which)

        @pl.when((plane > 0) & (core == 0))
        def _():
            sent(g_send.at[:, :, 0 : 2 * LANES], HALO_EVEN)

        @pl.when((plane > 0) & (core == 1))
        def _():
            sent(g_send.at[:, :, 0:LANES], HALO_ODD)

        received(gf_out, GF_OUT)
        received(gi_out, GI_ONE)


def per_device(inputs, grad_output, filter_taps, seqs, chans):
    rows, channels = inputs.shape
    lags, tap_channels = filter_taps.shape
    slots = ROW * chans
    group = channels // (slots * CORES)
    columns = CORES * ROW
    total_lags = lags * seqs
    tiles = total_lags // LANES
    window = total_lags + LANES
    one = pltpu.VMEM((slots, rows, LANES), BF16)
    two = pltpu.VMEM((CORES, group, ROW * LANES), BF16)
    return pl.pallas_call(
        kernel,
        out_shape=(
            jax.ShapeDtypeStruct(inputs.shape, BF16),
            jax.ShapeDtypeStruct(filter_taps.shape, F32),
        ),
        in_specs=[pl.BlockSpec(memory_space=pl.ANY)] * 3,
        out_specs=(pl.BlockSpec(memory_space=pl.ANY), pl.BlockSpec(memory_space=pl.ANY)),
        scratch_shapes=[
            one, one, two, two, two,
            pltpu.VMEM((CORES, group, 2 * LANES), BF16),
            two,
            pltpu.VMEM(filter_taps.shape, F32),
            pltpu.VMEM((columns, 8, LANES), F32),
            pltpu.VMEM((seqs, 8, LANES), F32),
            pltpu.VMEM((total_lags, LANES), F32),
            pltpu.VMEM((tiles, group, LANES), F32),
            pltpu.VMEM((group, 2 * SHORT, window), BF16),
            pltpu.VMEM(((2 * ROW + 3) * group, LANES), F32),
            pltpu.VMEM((2 * ROW * group, LANES), F32),
            pltpu.VMEM((group, SHORT, window), BF16),
            pltpu.VMEM((2 * ROW * group, LANES), F32),
            two, two, one,
            pltpu.VMEM((tiles, group * 8, LANES), F32),
            pltpu.VMEM((total_lags, LANES), F32),
            pltpu.VMEM((seqs, 8, LANES), F32),
            pltpu.VMEM((seqs, 8, LANES), F32),
            pltpu.VMEM(filter_taps.shape, F32),
            pltpu.SemaphoreType.DMA((12,)),
            pltpu.SemaphoreType.DMA((12,)),
        ],
        compiler_params=pltpu.CompilerParams(
            collective_id=0, has_side_effects=True, vmem_limit_bytes=48 * 1024 * 1024
        ),
    )(*(pltpu.with_memory_space_constraint(array, pltpu.HBM) for array in (inputs, grad_output, filter_taps)))


def solution(mesh):
    return jax.shard_map(
        functools.partial(per_device, seqs=mesh.shape["seq"], chans=mesh.shape["chan"]),
        mesh=mesh,
        in_specs=(P(("seq", "chan"), None), P(("seq", "chan"), None), P("seq", "chan")),
        out_specs=(P(("seq", "chan"), None), P("seq", "chan")),
        check_vma=False,
    )
```

time: 53.1 us -> 39.6 us (0.75)
  the two profiles are of different devices: /device:TPU:1 before, /device:TPU:2 now
where the time goes in v2:
time: 39.6 us; the launch traced here: 39.5 us
  Pallas kernels  37.6 us (95%)
  local copies, waits for them, and re-layouts  1.27 us (3%)
  between operations  0.64 us (2%)
    pallas_call x1, Pallas kernels, per_device(): pl.pallas_call(kernel, out_shape=(jax.ShapeDtypeStruct(inputs.shape, BF16...  37.6 us
    unnamed x2, local copies, waits for them, and re-layouts  1.27 us

profile of v2, /device:TPU:2, one launch (start us, length us, event | category | flops | bytes accessed | tf_op | source)
XLA Modules:
  0.0 39.5 jit_solution(4970612005503925665)
XLA Ops:
  0.6 37.6 %shard_map.50 = (bf16[16,4096]{1,0:T(8,128)(2,1)S(1)}, f32[12,512]{1,0:T(8,128)S(1)}) custom-call(bf16[16,4096]{1,0:T(8,128)(2,1)} %x_hbm.1, bf16[16,4096]{1,0:T(8,128)(2,1)} %g_hbm.1, f32[12,512]{1,0:T(8,128)} %taps_hbm.1), custom_call_target="tpu_custom_call" | custom-call | tf_op jit(solution)/shard_map/pallas_call | solution.py:396
  38.2 0.7 %copy.7 = bf16[16,4096]{1,0:T(8,128)(2,1)} copy(bf16[16,4096]{1,0:T(8,128)(2,1)S(1)} %get-tuple-element.4) | data formatting | bytes 262144
  38.9 0.6 %copy.8 = f32[12,512]{1,0:T(8,128)} copy(f32[12,512]{1,0:T(8,128)S(1)} %get-tuple-element.5) | data formatting | bytes 49152

commit v3 on v2

--- a/solution.py
+++ b/solution.py
@@ -18,7 +18,7 @@
 SHORT = 32
 FOLDS = LANES // SHORT
 
-G_ONE, X_ONE, TAPS, G_TWO, X_TWO, HALO_EVEN, HALO_ODD, GI_TWO, GI_ONE, GF, TAPS_IN, GF_OUT = range(12)
+G_ONE, X_ONE, TAPS, G_TWO, X_TWO, HALO_EVEN, HALO_ODD, GI_TWO, GI_ONE, GF, TAPS_IN, GF_OUT, G_IN, X_IN = range(14)
 
 
 def contract(lhs, rhs, lhs_dim, rhs_dim):
@@ -33,9 +33,9 @@
 
 def kernel(
     x_hbm, g_hbm, taps_hbm, gi_out, gf_out,
-    g_one, x_one, g_send, x_send, g_two, g_halo, x_two,
+    g_own, x_own, g_one, x_one, g_send, x_send, g_two, g_halo, x_two,
     taps, tap_send, tap_recv, tap_rows, tap_tiles, toeplitz,
-    g_wide, x_wide, g_cat, gi_wide, gi_send, gi_two, gi_turn,
+    g_wide, x_wide, gi_wide, gi_send, gi_two, gi_turn,
     gf_partial, gf_rows, gf_send, gf_recv, gf_own,
     send_sem, recv_sem,
 ):
@@ -56,6 +56,7 @@
     tap_count = tap_tiles.shape[0]
     group = tap_tiles.shape[1]
     rows_of_x = CORES * ROW
+    pitch = group
 
     def received(ref, which):
         pltpu.make_async_copy(ref, ref, recv_sem.at[which]).wait()
@@ -74,6 +75,8 @@
 
     with jax.named_scope("greet"):
         local(taps_hbm, taps, TAPS_IN)
+        local(g_hbm, g_own, G_IN)
+        local(x_hbm, x_own, X_IN)
         barrier = pltpu.get_barrier_semaphore()
 
         def greet_seq(step, carry):
@@ -113,6 +116,8 @@
     eye = (row == lane).astype(F32).astype(BF16)
     flip = (row + lane == LANES - 1).astype(F32).astype(BF16)
 
+    received(g_own, G_IN)
+    received(x_own, X_IN)
     with jax.named_scope("barrier"):
         pl.semaphore_wait(barrier, seqs - 1 + ROW * (chans - 1))
 
@@ -120,15 +125,24 @@
         start = lax.rem(index, chans) * (ROW * LANES) + lax.div(index, chans) * LANES
         return ref.at[:, pl.ds(pl.multiple_of(start, LANES), LANES)]
 
+    def for_others(count, body):
+        def step(first, carry):
+            for extra in range(1, 5):
+                body(first * 4 + extra)
+            return carry
+
+        lax.fori_loop(0, (count - 1) // 4, step, 0)
+        for shift in range((count - 1) // 4 * 4 + 1, count):
+            body(shift)
+
     def to_plane(src_of, dst, which):
-        def step(shift, carry):
+        def step(shift):
             index = slot + shift
             index = jnp.where(index >= slots, index - slots, index)
             to = (plane * ROW + lax.div(index, chans)) * CORES + core
             remote(src_of(index), dst, which, to, lax.rem(index, chans))
-            return carry
-
-        lax.fori_loop(1, slots, step, 0)
+
+        for_others(slots, step)
         local(src_of(slot), dst, which)
 
     def to_sibling(src, dst, which):
@@ -136,19 +150,18 @@
         local(src.at[core], dst.at[core], which)
 
     def to_seq(src_of, dst, which):
-        def step(shift, carry):
+        def step(shift):
             index = seq + shift
             index = jnp.where(index >= seqs, index - seqs, index)
             remote(src_of(index), dst, which, index, chan)
-            return carry
-
-        lax.fori_loop(1, seqs, step, 0)
+
+        for_others(seqs, step)
         local(src_of(seq), dst, which)
 
     with jax.named_scope("send_one"):
-        to_plane(functools.partial(columns_of, g_hbm), g_one.at[slot], G_ONE)
+        to_plane(functools.partial(columns_of, g_own), g_one.at[slot], G_ONE)
         to_seq(lambda index: tap_send.at[lax.rem(index, columns)], tap_recv.at[seq], TAPS)
-        to_plane(functools.partial(columns_of, x_hbm), x_one.at[slot], X_ONE)
+        to_plane(functools.partial(columns_of, x_own), x_one.at[slot], X_ONE)
 
     def turn(source, index):
         rows = source[chans * index : chans * (index + 1)].reshape(LANES, LANES)
@@ -186,15 +199,6 @@
             turned = contract(turn(x_one, index), flip, 1, 0).astype(BF16)
             x_send[:, :, index * LANES : (index + 1) * LANES] = by_core(turned)
         to_sibling(x_send, x_two, X_TWO)
-
-    with jax.named_scope("unpack_taps"):
-        received(tap_recv, TAPS)
-        for lag in range(half_lags):
-            rows = tap_recv[:, lag, :]
-            tap_rows[pl.ds(lag, seqs, stride=lags), :] = rows
-            tap_rows[pl.ds(half_lags + lag, seqs, stride=lags), :] = left(rows, HALF)
-        for tile in range(tap_count):
-            tap_tiles[tile] = tap_rows[tile * LANES : (tile + 1) * LANES, :].T[0:group, :]
 
     row = lax.broadcasted_iota(jnp.int32, (SHORT, LANES), 0)
     lane = lax.broadcasted_iota(jnp.int32, (SHORT, LANES), 1)
@@ -223,11 +227,20 @@
 
         lax.fori_loop(0, group // unroll, step, 0)
 
+    with jax.named_scope("unpack_taps"):
+        received(tap_recv, TAPS)
+        for lag in range(half_lags):
+            rows = tap_recv[:, lag, :]
+            tap_rows[pl.ds(lag, seqs, stride=lags), :] = rows
+            tap_rows[pl.ds(half_lags + lag, seqs, stride=lags), :] = left(rows, HALF)
+        for tile in range(tap_count):
+            tap_tiles[tile] = tap_rows[tile * LANES : (tile + 1) * LANES, :].T[0:group, :]
+
     with jax.named_scope("toeplitz"):
         for_channels(build, 16)
 
     def widen(source, target, index, from_core, at):
-        target[at * group : (at + 1) * group, :] = source[
+        target[at * pitch : at * pitch + group, :] = source[
             from_core, :, index * LANES : (index + 1) * LANES
         ].astype(F32)
 
@@ -247,15 +260,15 @@
 
         @pl.when(plane == PLANES - 1)
         def _():
-            g_wide[rows_of_x * group : (rows_of_x + 3) * group, :] = jnp.zeros((3 * group, LANES), F32)
+            g_wide[rows_of_x * pitch : (rows_of_x + 3) * pitch, :] = jnp.zeros((3 * pitch, LANES), F32)
 
     def strided(channel, blocks_ahead=0):
-        return pl.ds(channel + blocks_ahead * group, rows_of_x, stride=group)
+        return pl.ds(channel + blocks_ahead * pitch, rows_of_x, stride=pitch)
 
     lane_of_row = lax.broadcasted_iota(jnp.int32, (rows_of_x, LANES), 1)
     keep = lane - row < LANES - SHORT + 1
 
-    def window_step(channel):
+    def gradients_step(channel):
         blocks = [g_wide[strided(channel, tile), :] for tile in range(tap_count + 1)]
         folds = []
         for fold in range(FOLDS):
@@ -266,17 +279,22 @@
                     jnp.where(near_end, shifted[tile], shifted[tile + 1]) for tile in range(tap_count)
                 ] + [shifted[tap_count]]
             folds.append(jnp.concatenate(shifted, axis=1))
-        g_cat[channel] = jnp.concatenate(folds, axis=0).astype(BF16)
-
-    with jax.named_scope("windows"):
-        for_channels(window_step, 16)
-
-    def filter_step(channel):
+        windows = jnp.concatenate(folds, axis=0).astype(BF16)
+
+        result = contract(windows, toeplitz[channel], 1, 1)
+        result = jnp.concatenate([result, jnp.zeros((SHORT, LANES - 2 * SHORT), F32)], axis=1)
+        result = result + left(result, SHORT)
+        total = result[0:rows_of_x]
+        for fold in range(1, FOLDS):
+            part = pltpu.roll(result[fold * rows_of_x : (fold + 1) * rows_of_x], SHORT * fold, 1)
+            total = jnp.where(lane_of_row < SHORT * fold, total, part)
+        gi_wide[strided(channel), :] = total
+
         source = x_wide[strided(channel), :]
         mine = jnp.concatenate(
             [left(source, LANES - SHORT * (fold + 1)) for fold in range(FOLDS)], axis=0
         ).astype(BF16)
-        product = contract(mine[:, 0:SHORT], g_cat[channel], 0, 0)
+        product = contract(mine[:, 0:SHORT], windows, 0, 0)
         rolled = [
             pltpu.roll(
                 product[:, tile * LANES : (tile + 1) * LANES], LANES - SHORT + 1, 1, stride=1, stride_axis=0
@@ -288,56 +306,36 @@
             total = (total[0:8] + total[8:16]) + (total[16:24] + total[24:32])
             gf_partial[tile, pl.ds(pl.multiple_of(channel * 8, 8), 8), :] = total
 
-    def inputs_step(channel):
-        result = contract(g_cat[channel], toeplitz[channel], 1, 1)
-        result = jnp.concatenate([result, jnp.zeros((SHORT, LANES - 2 * SHORT), F32)], axis=1)
-        result = result + left(result, SHORT)
-        total = result[0:rows_of_x]
-        for fold in range(1, FOLDS):
-            part = pltpu.roll(result[fold * rows_of_x : (fold + 1) * rows_of_x], SHORT * fold, 1)
-            total = jnp.where(lane_of_row < SHORT * fold, total, part)
-        gi_wide[strided(channel), :] = total
-
-    filter_first = plane >= PLANES // 2
-    filter_turn = jnp.where(filter_first, 0, 1)
-
-    def two_turns(index, carry):
-        @pl.when(index == filter_turn)
-        def _():
-            received(x_two, X_TWO)
-            for place_from in range(ROW):
-                for from_core in range(CORES):
-                    widen(x_two, x_wide, place_from, from_core, CORES * place_from + from_core)
-            for_channels(filter_step, 8)
-            for tile in range(tap_count):
-                total = gf_partial[tile, pl.ds(0, group, stride=8), :]
-                for part in range(1, 8):
-                    total = total + gf_partial[tile, pl.ds(part, group, stride=8), :]
-                total = jnp.concatenate([total, jnp.zeros((LANES - group, LANES), F32)], axis=0)
-                gf_rows[tile * LANES : (tile + 1) * LANES, :] = total.T
-            for lag in range(half_lags):
-                early = gf_rows[pl.ds(lag, seqs, stride=lags), :]
-                late = gf_rows[pl.ds(half_lags + lag, seqs, stride=lags), :]
-                gf_send[:, lag, :] = early + left(late, HALF)
-            for lag in range(half_lags, 8):
-                gf_send[:, lag, :] = jnp.zeros((seqs, LANES), F32)
-            to_seq(lambda to: gf_send.at[to], gf_recv.at[seq], GF)
-
-        @pl.when(index != filter_turn)
-        def _():
-            for_channels(inputs_step, 16)
-            for place_to in range(ROW):
-                for to_core in range(CORES):
-                    start = (CORES * place_to + to_core) * group
-                    gi_send[to_core, :, place_to * LANES : (place_to + 1) * LANES] = gi_wide[
-                        start : start + group, :
-                    ].astype(BF16)
-            to_sibling(gi_send, gi_two, GI_TWO)
-
-        return carry
-
-    with jax.named_scope("both_gradients"):
-        lax.fori_loop(0, 2, two_turns, 0)
+    with jax.named_scope("widen_x"):
+        received(x_two, X_TWO)
+        for index in range(ROW):
+            for from_core in range(CORES):
+                widen(x_two, x_wide, index, from_core, CORES * index + from_core)
+
+    with jax.named_scope("gradients"):
+        for_channels(gradients_step, 16)
+
+    with jax.named_scope("send_gi_two"):
+        for index in range(ROW):
+            for to_core in range(CORES):
+                start = (CORES * index + to_core) * pitch
+                gi_send[to_core, :, index * LANES : (index + 1) * LANES] = gi_wide[start : start + group, :].astype(BF16)
+        to_sibling(gi_send, gi_two, GI_TWO)
+
+    with jax.named_scope("send_gf"):
+        for tile in range(tap_count):
+            total = gf_partial[tile, pl.ds(0, group, stride=8), :]
+            for part in range(1, 8):
+                total = total + gf_partial[tile, pl.ds(part, group, stride=8), :]
+            total = jnp.concatenate([total, jnp.zeros((LANES - group, LANES), F32)], axis=0)
+            gf_rows[tile * LANES : (tile + 1) * LANES, :] = total.T
+        for lag in range(half_lags):
+            early = gf_rows[pl.ds(lag, seqs, stride=lags), :]
+            late = gf_rows[pl.ds(half_lags + lag, seqs, stride=lags), :]
+            gf_send[:, lag, :] = early + left(late, HALF)
+        for lag in range(half_lags, 8):
+            gf_send[:, lag, :] = jnp.zeros((seqs, LANES), F32)
+        to_seq(lambda index: gf_send.at[index], gf_recv.at[seq], GF)
 
     with jax.named_scope("turn_gi"):
         received(gi_two, GI_TWO)
@@ -402,6 +400,8 @@
         in_specs=[pl.BlockSpec(memory_space=pl.ANY)] * 3,
         out_specs=(pl.BlockSpec(memory_space=pl.ANY), pl.BlockSpec(memory_space=pl.ANY)),
         scratch_shapes=[
+            pltpu.VMEM(inputs.shape, BF16),
+            pltpu.VMEM(inputs.shape, BF16),
             one, one, two, two, two,
             pltpu.VMEM((CORES, group, 2 * LANES), BF16),
             two,
@@ -413,7 +413,6 @@
             pltpu.VMEM((group, 2 * SHORT, window), BF16),
             pltpu.VMEM(((2 * ROW + 3) * group, LANES), F32),
             pltpu.VMEM((2 * ROW * group, LANES), F32),
-            pltpu.VMEM((group, SHORT, window), BF16),
             pltpu.VMEM((2 * ROW * group, LANES), F32),
             two, two, one,
             pltpu.VMEM((tiles, group * 8, LANES), F32),
@@ -421,8 +420,8 @@
             pltpu.VMEM((seqs, 8, LANES), F32),
             pltpu.VMEM((seqs, 8, LANES), F32),
             pltpu.VMEM(filter_taps.shape, F32),
-            pltpu.SemaphoreType.DMA((12,)),
-            pltpu.SemaphoreType.DMA((12,)),
+            pltpu.SemaphoreType.DMA((14,)),
+            pltpu.SemaphoreType.DMA((14,)),
         ],
         compiler_params=pltpu.CompilerParams(
             collective_id=0, has_side_effects=True, vmem_limit_bytes=48 * 1024 * 1024

time: 39.6 us -> 38.3 us (0.967)
  the two profiles are of different devices: /device:TPU:2 before, /device:TPU:1 now
where the time goes in v3:
time: 38.3 us; the launch traced here: 38.2 us
  Pallas kernels  36.3 us (95%)
  local copies, waits for them, and re-layouts  1.27 us (3%)
  between operations  0.64 us (2%)
    pallas_call x1, Pallas kernels, per_device(): pl.pallas_call(kernel, out_shape=(jax.ShapeDtypeStruct(inputs.shape, BF16...  36.3 us
    unnamed x2, local copies, waits for them, and re-layouts  1.27 us

profile of v3, /device:TPU:1, one launch (start us, length us, event | category | flops | bytes accessed | tf_op | source)
XLA Modules:
  0.0 38.2 jit_solution(9830355101768886601)
XLA Ops:
  0.6 36.3 %shard_map.50 = (bf16[16,4096]{1,0:T(8,128)(2,1)S(1)}, f32[12,512]{1,0:T(8,128)S(1)}) custom-call(bf16[16,4096]{1,0:T(8,128)(2,1)} %x_hbm.1, bf16[16,4096]{1,0:T(8,128)(2,1)} %g_hbm.1, f32[12,512]{1,0:T(8,128)} %taps_hbm.1), custom_call_target="tpu_custom_call" | custom-call | tf_op jit(solution)/shard_map/pallas_call | solution.py:394
  36.9 0.7 %copy.7 = bf16[16,4096]{1,0:T(8,128)(2,1)} copy(bf16[16,4096]{1,0:T(8,128)(2,1)S(1)} %get-tuple-element.4) | data formatting | bytes 262144
  37.6 0.6 %copy.8 = f32[12,512]{1,0:T(8,128)} copy(f32[12,512]{1,0:T(8,128)S(1)} %get-tuple-element.5) | data formatting | bytes 49152

commit v4 on v3

--- a/solution.py
+++ b/solution.py
@@ -17,6 +17,8 @@
 PLANES = 4
 SHORT = 32
 FOLDS = LANES // SHORT
+TOGETHER = 16
+LAGS = 1
 
 G_ONE, X_ONE, TAPS, G_TWO, X_TWO, HALO_EVEN, HALO_ODD, GI_TWO, GI_ONE, GF, TAPS_IN, GF_OUT, G_IN, X_IN = range(14)
 
@@ -32,11 +34,11 @@
 
 
 def kernel(
-    x_hbm, g_hbm, taps_hbm, gi_out, gf_out,
+    x_hbm, g_hbm, taps_hbm, gi_out, gf_recv,
     g_own, x_own, g_one, x_one, g_send, x_send, g_two, g_halo, x_two,
     taps, tap_send, tap_recv, tap_rows, tap_tiles, toeplitz,
     g_wide, x_wide, gi_wide, gi_send, gi_two, gi_turn,
-    gf_partial, gf_rows, gf_send, gf_recv, gf_own,
+    gf_partial, gf_rows, gf_send,
     send_sem, recv_sem,
 ):
     seqs = lax.axis_size("seq")
@@ -96,8 +98,10 @@
                 )
             return carry
 
-        lax.fori_loop(1, seqs, greet_seq, 0)
+        lax.fori_loop(8, 25, greet_seq, 0)
         lax.fori_loop(1, chans, greet_plane, 0)
+        lax.fori_loop(1, 8, greet_seq, 0)
+        lax.fori_loop(25, seqs, greet_seq, 0)
 
     first_half = lax.broadcasted_iota(jnp.int32, (8, LANES), 1) < HALF
 
@@ -160,7 +164,7 @@
 
     with jax.named_scope("send_one"):
         to_plane(functools.partial(columns_of, g_own), g_one.at[slot], G_ONE)
-        to_seq(lambda index: tap_send.at[lax.rem(index, columns)], tap_recv.at[seq], TAPS)
+        to_seq(lambda index: tap_send.at[lax.rem(index, columns), 0:half_lags], tap_recv.at[seq, 0:half_lags], TAPS)
         to_plane(functools.partial(columns_of, x_own), x_one.at[slot], X_ONE)
 
     def turn(source, index):
@@ -228,7 +232,7 @@
         lax.fori_loop(0, group // unroll, step, 0)
 
     with jax.named_scope("unpack_taps"):
-        received(tap_recv, TAPS)
+        received(tap_recv.at[:, 0:half_lags], TAPS)
         for lag in range(half_lags):
             rows = tap_recv[:, lag, :]
             tap_rows[pl.ds(lag, seqs, stride=lags), :] = rows
@@ -268,7 +272,7 @@
     lane_of_row = lax.broadcasted_iota(jnp.int32, (rows_of_x, LANES), 1)
     keep = lane - row < LANES - SHORT + 1
 
-    def gradients_step(channel):
+    def prepare(channel):
         blocks = [g_wide[strided(channel, tile), :] for tile in range(tap_count + 1)]
         folds = []
         for fold in range(FOLDS):
@@ -280,8 +284,16 @@
                 ] + [shifted[tap_count]]
             folds.append(jnp.concatenate(shifted, axis=1))
         windows = jnp.concatenate(folds, axis=0).astype(BF16)
-
-        result = contract(windows, toeplitz[channel], 1, 1)
+        source = x_wide[strided(channel), :]
+        mine = jnp.concatenate(
+            [left(source, LANES - SHORT * (fold + 1)) for fold in range(FOLDS)], axis=0
+        ).astype(BF16)
+        return windows, mine[:, 0:SHORT]
+
+    def multiply(channel, windows, mine):
+        return contract(windows, toeplitz[channel], 1, 1), contract(mine, windows, 0, 0)
+
+    def finish(channel, result, product):
         result = jnp.concatenate([result, jnp.zeros((SHORT, LANES - 2 * SHORT), F32)], axis=1)
         result = result + left(result, SHORT)
         total = result[0:rows_of_x]
@@ -289,12 +301,6 @@
             part = pltpu.roll(result[fold * rows_of_x : (fold + 1) * rows_of_x], SHORT * fold, 1)
             total = jnp.where(lane_of_row < SHORT * fold, total, part)
         gi_wide[strided(channel), :] = total
-
-        source = x_wide[strided(channel), :]
-        mine = jnp.concatenate(
-            [left(source, LANES - SHORT * (fold + 1)) for fold in range(FOLDS)], axis=0
-        ).astype(BF16)
-        product = contract(mine[:, 0:SHORT], windows, 0, 0)
         rolled = [
             pltpu.roll(
                 product[:, tile * LANES : (tile + 1) * LANES], LANES - SHORT + 1, 1, stride=1, stride_axis=0
@@ -306,6 +312,19 @@
             total = (total[0:8] + total[8:16]) + (total[16:24] + total[24:32])
             gf_partial[tile, pl.ds(pl.multiple_of(channel * 8, 8), 8), :] = total
 
+    def gradients_group(first, carry):
+        ready, done = {}, {}
+        for step in range(TOGETHER + 2 * LAGS):
+            if step < TOGETHER:
+                ready[step] = prepare(first * TOGETHER + step)
+            index = step - LAGS
+            if 0 <= index < TOGETHER:
+                done[index] = multiply(first * TOGETHER + index, *ready.pop(index))
+            index = step - 2 * LAGS
+            if 0 <= index < TOGETHER:
+                finish(first * TOGETHER + index, *done.pop(index))
+        return carry
+
     with jax.named_scope("widen_x"):
         received(x_two, X_TWO)
         for index in range(ROW):
@@ -313,7 +332,7 @@
                 widen(x_two, x_wide, index, from_core, CORES * index + from_core)
 
     with jax.named_scope("gradients"):
-        for_channels(gradients_step, 16)
+        lax.fori_loop(0, group // TOGETHER, gradients_group, 0)
 
     with jax.named_scope("send_gi_two"):
         for index in range(ROW):
@@ -335,7 +354,7 @@
             gf_send[:, lag, :] = early + left(late, HALF)
         for lag in range(half_lags, 8):
             gf_send[:, lag, :] = jnp.zeros((seqs, LANES), F32)
-        to_seq(lambda index: gf_send.at[index], gf_recv.at[seq], GF)
+        to_seq(lambda index: gf_send.at[index, 0:half_lags], gf_recv.at[seq, 0:half_lags], GF)
 
     with jax.named_scope("turn_gi"):
         received(gi_two, GI_TWO)
@@ -345,26 +364,10 @@
             gi_turn[chans * index : chans * (index + 1)] = turned.reshape(chans, LANES // chans, LANES)
         to_plane(lambda index: gi_turn.at[index], columns_of(gi_out, slot), GI_ONE)
 
-    with jax.named_scope("unpack_gf"):
-        received(gf_recv, GF)
-        sums = []
-        for index in range(columns):
-            total = gf_recv[index]
-            for other in range(1, PLANES):
-                total = total + gf_recv[other * columns + index]
-            sums.append(total)
-        for tile in range(columns // 2):
-            lanes = slice(tile * LANES, (tile + 1) * LANES)
-            early = jnp.where(first_half, sums[2 * tile], left(sums[2 * tile + 1], HALF))
-            late = jnp.where(first_half, left(sums[2 * tile], HALF), sums[2 * tile + 1])
-            gf_own[0:half_lags, lanes] = early[0:half_lags]
-            gf_own[half_lags:lags, lanes] = late[0:half_lags]
-        local(gf_own, gf_out, GF_OUT)
-
     with jax.named_scope("finish"):
         for ref, which in (
-            (g_one, G_ONE), (x_one, X_ONE), (tap_recv, TAPS), (g_send, G_TWO), (x_send, X_TWO),
-            (gi_send, GI_TWO), (gi_turn, GI_ONE), (gf_send, GF),
+            (g_one, G_ONE), (x_one, X_ONE), (tap_recv.at[:, 0:half_lags], TAPS), (g_send, G_TWO), (x_send, X_TWO),
+            (gi_send, GI_TWO), (gi_turn, GI_ONE), (gf_send.at[:, 0:half_lags], GF),
         ):
             sent(ref.at[pl.ds(0, ref.shape[0] - 1)], which)
 
@@ -376,8 +379,31 @@
         def _():
             sent(g_send.at[:, :, 0:LANES], HALO_ODD)
 
-        received(gf_out, GF_OUT)
+        received(gf_recv.at[:, 0:half_lags], GF)
         received(gi_out, GI_ONE)
+
+
+def gather_outputs(columns, gi_ref, gf_ref, gi_out, gf_out, gf_own, sem):
+    copy = pltpu.make_async_copy(gi_ref, gi_out, sem.at[0])
+    copy.start()
+    first_half = lax.broadcasted_iota(jnp.int32, (8, LANES), 1) < HALF
+    half_lags = gf_own.shape[0] // 2
+    sums = []
+    for index in range(columns):
+        total = gf_ref[index]
+        for other in range(1, PLANES):
+            total = total + gf_ref[other * columns + index]
+        sums.append(total)
+    for tile in range(columns // 2):
+        lanes = slice(tile * LANES, (tile + 1) * LANES)
+        early = jnp.where(first_half, sums[2 * tile], left(sums[2 * tile + 1], HALF))
+        late = jnp.where(first_half, left(sums[2 * tile], HALF), sums[2 * tile + 1])
+        gf_own[0:half_lags, lanes] = early[0:half_lags]
+        gf_own[half_lags : 2 * half_lags, lanes] = late[0:half_lags]
+    gf_copy = pltpu.make_async_copy(gf_own, gf_out, sem.at[1])
+    gf_copy.start()
+    copy.wait()
+    gf_copy.wait()
 
 
 def per_device(inputs, grad_output, filter_taps, seqs, chans):
@@ -391,11 +417,11 @@
     window = total_lags + LANES
     one = pltpu.VMEM((slots, rows, LANES), BF16)
     two = pltpu.VMEM((CORES, group, ROW * LANES), BF16)
-    return pl.pallas_call(
+    gi_parts, gf_parts = pl.pallas_call(
         kernel,
         out_shape=(
             jax.ShapeDtypeStruct(inputs.shape, BF16),
-            jax.ShapeDtypeStruct(filter_taps.shape, F32),
+            jax.ShapeDtypeStruct((seqs, 8, LANES), F32),
         ),
         in_specs=[pl.BlockSpec(memory_space=pl.ANY)] * 3,
         out_specs=(pl.BlockSpec(memory_space=pl.ANY), pl.BlockSpec(memory_space=pl.ANY)),
@@ -418,8 +444,6 @@
             pltpu.VMEM((tiles, group * 8, LANES), F32),
             pltpu.VMEM((total_lags, LANES), F32),
             pltpu.VMEM((seqs, 8, LANES), F32),
-            pltpu.VMEM((seqs, 8, LANES), F32),
-            pltpu.VMEM(filter_taps.shape, F32),
             pltpu.SemaphoreType.DMA((14,)),
             pltpu.SemaphoreType.DMA((14,)),
         ],
@@ -427,6 +451,17 @@
             collective_id=0, has_side_effects=True, vmem_limit_bytes=48 * 1024 * 1024
         ),
     )(*(pltpu.with_memory_space_constraint(array, pltpu.HBM) for array in (inputs, grad_output, filter_taps)))
+    return pl.pallas_call(
+        functools.partial(gather_outputs, columns),
+        out_shape=(
+            jax.ShapeDtypeStruct(inputs.shape, BF16),
+            jax.ShapeDtypeStruct(filter_taps.shape, F32),
+        ),
+        in_specs=[pl.BlockSpec(memory_space=pltpu.VMEM)] * 2,
+        out_specs=(pl.BlockSpec(memory_space=pltpu.HBM), pl.BlockSpec(memory_space=pltpu.HBM)),
+        scratch_shapes=[pltpu.VMEM(filter_taps.shape, F32), pltpu.SemaphoreType.DMA((2,))],
+        compiler_params=pltpu.CompilerParams(vmem_limit_bytes=16 * 1024 * 1024),
+    )(gi_parts, gf_parts)
 
 
 def solution(mesh):

time: 38.3 us -> 36.1 us (0.943)
  local copies, waits for them, and re-layouts: 1.27 us -> 0 us
  Pallas kernels: 36.3 us -> 35.4 us
    pallas_call x1, Pallas kernels: 36.3 us -> 34.7 us  [per_device(): pl.pallas_call(kernel, out_shape=(jax.ShapeDtypeStruct(inputs.shape, BF16...]
    unnamed x2 -> x0, local copies, waits for them, and re-layouts: 1.27 us -> none
    pallas_call x0 -> x1, Pallas kernels: none -> 0.71 us  [per_device(): pl.pallas_call(functools.partial(gather_outputs, columns), out_shape=(jax...]
where the time goes in v4:
time: 36.1 us; the launch traced here: 36 us
  Pallas kernels  35.4 us (98%)
  between operations  0.64 us (2%)
    pallas_call x1, Pallas kernels, per_device(): pl.pallas_call(kernel, out_shape=(jax.ShapeDtypeStruct(inputs.shape, BF16...  34.7 us

profile of v4, /device:TPU:1, one launch (start us, length us, event | category | flops | bytes accessed | tf_op | source)
XLA Modules:
  0.0 36.0 jit_solution(18198633905877532753)
XLA Ops:
  0.6 34.7 %shard_map.50 = (bf16[16,4096]{1,0:T(8,128)(2,1)S(1)}, f32[32,8,128]{2,1,0:T(8,128)S(1)}) custom-call(bf16[16,4096]{1,0:T(8,128)(2,1)} %x_hbm.1, bf16[16,4096]{1,0:T(8,128)(2,1)} %g_hbm.1, f32[12,512]{1,0:T(8,128)} %taps_hbm.1), custom_call_target="tpu_custom_call" | custom-call | tf_op jit(solution)/shard_map/pallas_call | solution.py:420
  35.3 0.7 %shard_map.51 = (bf16[16,4096]{1,0:T(8,128)(2,1)}, f32[12,512]{1,0:T(8,128)}) custom-call(bf16[16,4096]{1,0:T(8,128)(2,1)S(1)} %get-tuple-element.4.gi_ref, f32[32,8,128]{2,1,0:T(8,128)S(1)} %get-tuple-element.5.gf_ref), custom_call_target="tpu_custom_call" | custom-call | tf_op jit(solution)/shard_map/pallas_call | solution.py:454

commit v5 on v4

--- a/solution.py
+++ b/solution.py
@@ -17,8 +17,7 @@
 PLANES = 4
 SHORT = 32
 FOLDS = LANES // SHORT
-TOGETHER = 16
-LAGS = 1
+LAGS = 2
 
 G_ONE, X_ONE, TAPS, G_TWO, X_TWO, HALO_EVEN, HALO_ODD, GI_TWO, GI_ONE, GF, TAPS_IN, GF_OUT, G_IN, X_IN = range(14)
 
@@ -37,7 +36,7 @@
     x_hbm, g_hbm, taps_hbm, gi_out, gf_recv,
     g_own, x_own, g_one, x_one, g_send, x_send, g_two, g_halo, x_two,
     taps, tap_send, tap_recv, tap_rows, tap_tiles, toeplitz,
-    g_wide, x_wide, gi_wide, gi_send, gi_two, gi_turn,
+    g_wide, x_wide, g_cat, x_cat, gi_wide, gi_send, gi_two, gi_turn,
     gf_partial, gf_rows, gf_send,
     send_sem, recv_sem,
 ):
@@ -241,7 +240,7 @@
             tap_tiles[tile] = tap_rows[tile * LANES : (tile + 1) * LANES, :].T[0:group, :]
 
     with jax.named_scope("toeplitz"):
-        for_channels(build, 16)
+        for_channels(build, 64)
 
     def widen(source, target, index, from_core, at):
         target[at * pitch : at * pitch + group, :] = source[
@@ -272,9 +271,8 @@
     lane_of_row = lax.broadcasted_iota(jnp.int32, (rows_of_x, LANES), 1)
     keep = lane - row < LANES - SHORT + 1
 
-    def prepare(channel):
+    def cut_windows(channel):
         blocks = [g_wide[strided(channel, tile), :] for tile in range(tap_count + 1)]
-        folds = []
         for fold in range(FOLDS):
             shifted = [left(values, SHORT * fold) for values in blocks]
             if fold > 0:
@@ -282,18 +280,24 @@
                 shifted = [
                     jnp.where(near_end, shifted[tile], shifted[tile + 1]) for tile in range(tap_count)
                 ] + [shifted[tap_count]]
-            folds.append(jnp.concatenate(shifted, axis=1))
-        windows = jnp.concatenate(folds, axis=0).astype(BF16)
+            if fold % 2 == 0:
+                before = shifted
+                continue
+            for tile in range(tap_count + 1):
+                g_cat[channel, (fold - 1) * rows_of_x : (fold + 1) * rows_of_x, tile * LANES : (tile + 1) * LANES] = (
+                    jnp.concatenate([before[tile], shifted[tile]], axis=0).astype(BF16)
+                )
+
+    def cut_x(channel):
         source = x_wide[strided(channel), :]
-        mine = jnp.concatenate(
+        x_cat[channel] = jnp.concatenate(
             [left(source, LANES - SHORT * (fold + 1)) for fold in range(FOLDS)], axis=0
         ).astype(BF16)
-        return windows, mine[:, 0:SHORT]
-
-    def multiply(channel, windows, mine):
-        return contract(windows, toeplitz[channel], 1, 1), contract(mine, windows, 0, 0)
-
-    def finish(channel, result, product):
+
+    def multiply_taps(channel):
+        return contract(g_cat[channel], toeplitz[channel], 1, 1)
+
+    def finish_inputs(channel, result):
         result = jnp.concatenate([result, jnp.zeros((SHORT, LANES - 2 * SHORT), F32)], axis=1)
         result = result + left(result, SHORT)
         total = result[0:rows_of_x]
@@ -301,6 +305,11 @@
             part = pltpu.roll(result[fold * rows_of_x : (fold + 1) * rows_of_x], SHORT * fold, 1)
             total = jnp.where(lane_of_row < SHORT * fold, total, part)
         gi_wide[strided(channel), :] = total
+
+    def multiply_x(channel):
+        return contract(x_cat[channel, :, 0:SHORT], g_cat[channel], 0, 0)
+
+    def finish_filter(channel, product):
         rolled = [
             pltpu.roll(
                 product[:, tile * LANES : (tile + 1) * LANES], LANES - SHORT + 1, 1, stride=1, stride_axis=0
@@ -312,27 +321,23 @@
             total = (total[0:8] + total[8:16]) + (total[16:24] + total[24:32])
             gf_partial[tile, pl.ds(pl.multiple_of(channel * 8, 8), 8), :] = total
 
-    def gradients_group(first, carry):
-        ready, done = {}, {}
-        for step in range(TOGETHER + 2 * LAGS):
-            if step < TOGETHER:
-                ready[step] = prepare(first * TOGETHER + step)
-            index = step - LAGS
-            if 0 <= index < TOGETHER:
-                done[index] = multiply(first * TOGETHER + index, *ready.pop(index))
-            index = step - 2 * LAGS
-            if 0 <= index < TOGETHER:
-                finish(first * TOGETHER + index, *done.pop(index))
-        return carry
-
-    with jax.named_scope("widen_x"):
-        received(x_two, X_TWO)
-        for index in range(ROW):
-            for from_core in range(CORES):
-                widen(x_two, x_wide, index, from_core, CORES * index + from_core)
-
-    with jax.named_scope("gradients"):
-        lax.fori_loop(0, group // TOGETHER, gradients_group, 0)
+    def pipelined(multiply, finish, together):
+        def step(first, carry):
+            done = {}
+            for index in range(together + LAGS):
+                if index < together:
+                    done[index] = multiply(first * together + index)
+                if index >= LAGS:
+                    finish(first * together + index - LAGS, done.pop(index - LAGS))
+            return carry
+
+        lax.fori_loop(0, group // together, step, 0)
+
+    with jax.named_scope("windows"):
+        for_channels(cut_windows, 32)
+
+    with jax.named_scope("grad_inputs"):
+        pipelined(multiply_taps, finish_inputs, 64)
 
     with jax.named_scope("send_gi_two"):
         for index in range(ROW):
@@ -340,6 +345,18 @@
                 start = (CORES * index + to_core) * pitch
                 gi_send[to_core, :, index * LANES : (index + 1) * LANES] = gi_wide[start : start + group, :].astype(BF16)
         to_sibling(gi_send, gi_two, GI_TWO)
+
+    with jax.named_scope("widen_x"):
+        received(x_two, X_TWO)
+        for index in range(ROW):
+            for from_core in range(CORES):
+                widen(x_two, x_wide, index, from_core, CORES * index + from_core)
+
+    with jax.named_scope("cut_x"):
+        for_channels(cut_x, 32)
+
+    with jax.named_scope("grad_filter"):
+        pipelined(multiply_x, finish_filter, 32)
 
     with jax.named_scope("send_gf"):
         for tile in range(tap_count):
@@ -439,6 +456,8 @@
             pltpu.VMEM((group, 2 * SHORT, window), BF16),
             pltpu.VMEM(((2 * ROW + 3) * group, LANES), F32),
             pltpu.VMEM((2 * ROW * group, LANES), F32),
+            pltpu.VMEM((group, SHORT, window), BF16),
+            pltpu.VMEM((group, SHORT, LANES), BF16),
             pltpu.VMEM((2 * ROW * group, LANES), F32),
             two, two, one,
             pltpu.VMEM((tiles, group * 8, LANES), F32),

time: 36.1 us -> 34.5 us (0.956)
  Pallas kernels: 35.4 us -> 33.7 us
    pallas_call x1, Pallas kernels: 34.7 us -> 33 us  [per_device(): pl.pallas_call(kernel, out_shape=(jax.ShapeDtypeStruct(inputs.shape, BF16...]
where the time goes in v5:
time: 34.5 us; the launch traced here: 34.4 us
  Pallas kernels  33.7 us (98%)
  between operations  0.64 us (2%)
    pallas_call x1, Pallas kernels, per_device(): pl.pallas_call(kernel, out_shape=(jax.ShapeDtypeStruct(inputs.shape, BF16...  33 us
    pallas_call x1, Pallas kernels, per_device(): pl.pallas_call(functools.partial(gather_outputs, columns), out_shape=(jax...  0.71 us

profile of v5, /device:TPU:1, one launch (start us, length us, event | category | flops | bytes accessed | tf_op | source)
XLA Modules:
  0.0 34.4 jit_solution(17194338168919717999)
XLA Ops:
  0.6 33.0 %shard_map.50 = (bf16[16,4096]{1,0:T(8,128)(2,1)S(1)}, f32[32,8,128]{2,1,0:T(8,128)S(1)}) custom-call(bf16[16,4096]{1,0:T(8,128)(2,1)} %x_hbm.1, bf16[16,4096]{1,0:T(8,128)(2,1)} %g_hbm.1, f32[12,512]{1,0:T(8,128)} %taps_hbm.1), custom_call_target="tpu_custom_call" | custom-call | tf_op jit(solution)/shard_map/pallas_call | solution.py:437
  33.7 0.7 %shard_map.51 = (bf16[16,4096]{1,0:T(8,128)(2,1)}, f32[12,512]{1,0:T(8,128)}) custom-call(bf16[16,4096]{1,0:T(8,128)(2,1)S(1)} %get-tuple-element.4.gi_ref, f32[32,8,128]{2,1,0:T(8,128)S(1)} %get-tuple-element.5.gf_ref), custom_call_target="tpu_custom_call" | custom-call | tf_op jit(solution)/shard_map/pallas_call | solution.py:473

commit v6 on v5

--- a/solution.py
+++ b/solution.py
@@ -129,13 +129,7 @@
         return ref.at[:, pl.ds(pl.multiple_of(start, LANES), LANES)]
 
     def for_others(count, body):
-        def step(first, carry):
-            for extra in range(1, 5):
-                body(first * 4 + extra)
-            return carry
-
-        lax.fori_loop(0, (count - 1) // 4, step, 0)
-        for shift in range((count - 1) // 4 * 4 + 1, count):
+        for shift in range(1, count):
             body(shift)
 
     def to_plane(src_of, dst, which):
@@ -295,11 +289,12 @@
         ).astype(BF16)
 
     def multiply_taps(channel):
-        return contract(g_cat[channel], toeplitz[channel], 1, 1)
+        windows = g_cat[channel]
+        high = contract(windows, toeplitz[channel, 0:SHORT, :], 1, 1)
+        return high + contract(windows, toeplitz[channel, SHORT : 2 * SHORT, :], 1, 1)
 
     def finish_inputs(channel, result):
-        result = jnp.concatenate([result, jnp.zeros((SHORT, LANES - 2 * SHORT), F32)], axis=1)
-        result = result + left(result, SHORT)
+        result = jnp.concatenate([result, jnp.zeros((SHORT, LANES - SHORT), F32)], axis=1)
         total = result[0:rows_of_x]
         for fold in range(1, FOLDS):
             part = pltpu.roll(result[fold * rows_of_x : (fold + 1) * rows_of_x], SHORT * fold, 1)
@@ -356,7 +351,7 @@
         for_channels(cut_x, 32)
 
     with jax.named_scope("grad_filter"):
-        pipelined(multiply_x, finish_filter, 32)
+        pipelined(multiply_x, finish_filter, 64)
 
     with jax.named_scope("send_gf"):
         for tile in range(tap_count):

time: 34.5 us -> 34.1 us (0.988)
  Pallas kernels: 33.7 us -> 33.3 us
    pallas_call x1, Pallas kernels: 33 us -> 32.6 us  [per_device(): pl.pallas_call(kernel, out_shape=(jax.ShapeDtypeStruct(inputs.shape, BF16...]
where the time goes in v6:
time: 34.1 us; the launch traced here: 34 us
  Pallas kernels  33.3 us (98%)
  between operations  0.64 us (2%)
    pallas_call x1, Pallas kernels, per_device(): pl.pallas_call(kernel, out_shape=(jax.ShapeDtypeStruct(inputs.shape, BF16...  32.6 us
    pallas_call x1, Pallas kernels, per_device(): pl.pallas_call(functools.partial(gather_outputs, columns), out_shape=(jax...  0.71 us

profile of v6, /device:TPU:1, one launch (start us, length us, event | category | flops | bytes accessed | tf_op | source)
XLA Modules:
  0.0 34.0 jit_solution(7936456633242185923)
XLA Ops:
  0.6 32.6 %shard_map.50 = (bf16[16,4096]{1,0:T(8,128)(2,1)S(1)}, f32[32,8,128]{2,1,0:T(8,128)S(1)}) custom-call(bf16[16,4096]{1,0:T(8,128)(2,1)} %x_hbm.1, bf16[16,4096]{1,0:T(8,128)(2,1)} %g_hbm.1, f32[12,512]{1,0:T(8,128)} %taps_hbm.1), custom_call_target="tpu_custom_call" | custom-call | tf_op jit(solution)/shard_map/pallas_call | solution.py:432
  33.2 0.7 %shard_map.51 = (bf16[16,4096]{1,0:T(8,128)(2,1)}, f32[12,512]{1,0:T(8,128)}) custom-call(bf16[16,4096]{1,0:T(8,128)(2,1)S(1)} %get-tuple-element.4.gi_ref, f32[32,8,128]{2,1,0:T(8,128)S(1)} %get-tuple-element.5.gf_ref), custom_call_target="tpu_custom_call" | custom-call | tf_op jit(solution)/shard_map/pallas_call | solution.py:468

commit v7 on v6

--- a/solution.py
+++ b/solution.py
@@ -348,7 +348,7 @@
                 widen(x_two, x_wide, index, from_core, CORES * index + from_core)
 
     with jax.named_scope("cut_x"):
-        for_channels(cut_x, 32)
+        for_channels(cut_x, 64)
 
     with jax.named_scope("grad_filter"):
         pipelined(multiply_x, finish_filter, 64)
@@ -446,17 +446,17 @@
             pltpu.VMEM(filter_taps.shape, F32),
             pltpu.VMEM((columns, 8, LANES), F32),
             pltpu.VMEM((seqs, 8, LANES), F32),
-            pltpu.VMEM((total_lags, LANES), F32),
+            pltpu.VMEM((total_lags + 16, LANES), F32),
             pltpu.VMEM((tiles, group, LANES), F32),
             pltpu.VMEM((group, 2 * SHORT, window), BF16),
-            pltpu.VMEM(((2 * ROW + 3) * group, LANES), F32),
-            pltpu.VMEM((2 * ROW * group, LANES), F32),
+            pltpu.VMEM(((2 * ROW + 4) * group, LANES), F32),
+            pltpu.VMEM(((2 * ROW + 1) * group, LANES), F32),
             pltpu.VMEM((group, SHORT, window), BF16),
             pltpu.VMEM((group, SHORT, LANES), BF16),
-            pltpu.VMEM((2 * ROW * group, LANES), F32),
+            pltpu.VMEM(((2 * ROW + 1) * group, LANES), F32),
             two, two, one,
-            pltpu.VMEM((tiles, group * 8, LANES), F32),
-            pltpu.VMEM((total_lags, LANES), F32),
+            pltpu.VMEM((tiles, group * 8 + 8, LANES), F32),
+            pltpu.VMEM((total_lags + 16, LANES), F32),
             pltpu.VMEM((seqs, 8, LANES), F32),
             pltpu.SemaphoreType.DMA((14,)),
             pltpu.SemaphoreType.DMA((14,)),

time: 34.1 us -> 34 us (level)
  no operation moved by 1% of the time
where the time goes in v7:
time: 34 us; the launch traced here: 33.9 us
  Pallas kernels  33.3 us (98%)
  between operations  0.64 us (2%)
    pallas_call x1, Pallas kernels, per_device(): pl.pallas_call(kernel, out_shape=(jax.ShapeDtypeStruct(inputs.shape, BF16...  32.5 us
    pallas_call x1, Pallas kernels, per_device(): pl.pallas_call(functools.partial(gather_outputs, columns), out_shape=(jax...  0.71 us

profile of v7, /device:TPU:1, one launch (start us, length us, event | category | flops | bytes accessed | tf_op | source)
XLA Modules:
  0.0 33.9 jit_solution(15370243298180912428)
XLA Ops:
  0.6 32.5 %shard_map.50 = (bf16[16,4096]{1,0:T(8,128)(2,1)S(1)}, f32[32,8,128]{2,1,0:T(8,128)S(1)}) custom-call(bf16[16,4096]{1,0:T(8,128)(2,1)} %x_hbm.1, bf16[16,4096]{1,0:T(8,128)(2,1)} %g_hbm.1, f32[12,512]{1,0:T(8,128)} %taps_hbm.1), custom_call_target="tpu_custom_call" | custom-call | tf_op jit(solution)/shard_map/pallas_call | solution.py:432
  33.2 0.7 %shard_map.51 = (bf16[16,4096]{1,0:T(8,128)(2,1)}, f32[12,512]{1,0:T(8,128)}) custom-call(bf16[16,4096]{1,0:T(8,128)(2,1)S(1)} %get-tuple-element.4.gi_ref, f32[32,8,128]{2,1,0:T(8,128)S(1)} %get-tuple-element.5.gf_ref), custom_call_target="tpu_custom_call" | custom-call | tf_op jit(solution)/shard_map/pallas_call | solution.py:468
